TPU v7x, 32 devices: a whole 2x2x4 slice. The times are simulated.
32 devices in a mesh: dp: 4 (over y, core), fsdp: 8 (over z, x).
Axes of the slice: x: 2, y: 2, z: 4, core: 2. Of those that a mesh axis runs over, the one named last changes fastest.
Arguments:
- inputs: bfloat16 [256, 324, 256], P(('dp', 'fsdp')), may hold values from -6 to 6
- classes: int32 [256], P(('dp', 'fsdp')), may hold values from 0 to 2
- offset_table: int32 [3, 324, 324], replicated, may hold values from 0 to 323, as said below
- bias_table: float32 [4, 324], replicated, may hold values from -5 to 5
- qkv_weight: bfloat16 [256, 768], P('fsdp'), may hold values from -0.375 to 0.375
- qkv_gain: bfloat16 [768], P('fsdp'), may hold values from 0.5 to 1.5
- qkv_shift: bfloat16 [768], P('fsdp'), may hold values from -3 to 3
- out_weight: bfloat16 [512, 256], P('fsdp'), may hold values from -0.25 to 0.25
- out_gain: bfloat16 [256], P('fsdp'), may hold values from 0.5 to 1.5
- out_shift: bfloat16 [256], P('fsdp'), may hold values from -3 to 3
- up_weight: bfloat16 [256, 512], P('fsdp'), may hold values from -0.375 to 0.375
- up_gain: bfloat16 [512], P('fsdp'), may hold values from 0.5 to 1.5
- up_shift: bfloat16 [512], P('fsdp'), may hold values from -3 to 3
- down_weight: bfloat16 [512, 256], P('fsdp'), may hold values from -0.25 to 0.25
- down_gain: bfloat16 [256], P('fsdp'), may hold values from 0.5 to 1.5
- down_shift: bfloat16 [256], P('fsdp'), may hold values from -3 to 3
- cotangent: bfloat16 [256, 324, 256], P(('dp', 'fsdp')), may hold values from -6 to 6
Outputs:
- output: bfloat16 [256, 324, 256], P(('dp', 'fsdp'))
- input_grad: float32 [256, 324, 256], P(('dp', 'fsdp'))
- table_grad: float32 [4, 324], replicated
- qkv_weight_grad: float32 [256, 768], P('fsdp')
- qkv_gain_grad: float32 [768], P('fsdp')
- qkv_shift_grad: float32 [768], P('fsdp')
- out_weight_grad: float32 [512, 256], P('fsdp')
- out_gain_grad: float32 [256], P('fsdp')
- out_shift_grad: float32 [256], P('fsdp')
- up_weight_grad: float32 [256, 512], P('fsdp')
- up_gain_grad: float32 [512], P('fsdp')
- up_shift_grad: float32 [512], P('fsdp')
- down_weight_grad: float32 [512, 256], P('fsdp')
- down_gain_grad: float32 [256], P('fsdp')
- down_shift_grad: float32 [256], P('fsdp')
Inputs may be any that keep to these rules, and one draw needn't show every extreme that they name: For class c of side s in (10, 14, 18) and n = s*s, the first n slots of an image hold the grid's cells in an order drawn per class; offset_table[c, q, p] = |row_q - row_p| * 18 + |col_q - col_p| for q, p < n and 0 elsewhere.
All inputs are finite; a program needn't handle non-finite values.
Results may differ from a plain program's by a relative error of at most 0.03.
Values may be sent and summed in bfloat16 or wider, within the bound.
A program may use at most 320 MiB of HBM per device.

v0:
```python
import jax
import jax.numpy as jnp
from jax import lax
from jax.sharding import PartitionSpec as P

HEADS = 4
KEY = 32
VALD = 128
GRID = 18
CLASSES = 3
SLOT = 324
NOFF = 324


EPS = 1e-05


def silu_slope(value):
    sigma = jax.nn.sigmoid(value)
    return sigma * (1.0 + value * (1.0 - sigma))


def norm_forward(value, weights, gain, shift):
    sums = lax.psum(
        (
            jnp.sum(value * weights, axis=0),
            jnp.sum(value * value * weights, axis=0),
            jnp.sum(weights),
        ),
        ("dp", "fsdp"),
    )
    total = sums[2]
    center = sums[0] / total
    square = sums[1] / total
    scale = lax.rsqrt(square - center * center + EPS)
    normed = (value - center) * scale
    return (normed * gain.astype(jnp.float32) + shift.astype(jnp.float32), normed, scale, total)


def norm_backward(grad, normed, scale, total, gain, weights):
    sums = lax.psum((jnp.sum(grad, axis=0), jnp.sum(grad * normed, axis=0)), ("dp", "fsdp"))
    shift_grad = sums[0]
    gain_grad = sums[1]
    gain_f = gain.astype(jnp.float32)
    inner = gain_f * (shift_grad + normed * gain_grad) / total
    return (scale * (grad * gain_f - weights * inner), gain_grad, shift_grad)


def attention_scores(query, keys, bias, keep):
    dots = jnp.einsum("iqhk,iphk->ihqp", query, keys, preferred_element_type=jnp.float32)
    scores = dots * KEY ** (-0.5) + bias
    return jnp.where(keep[:, None, None, :] > 0, scores, -1e30)


def left_product(left, right):
    return jnp.einsum("na,nb->ab", left, right, preferred_element_type=jnp.float32)


def right_product(left, right):
    return jnp.einsum("nb,ab->na", left, right, preferred_element_type=jnp.float32)


def own_slice(vector):
    width = vector.shape[0] // lax.axis_size("fsdp")
    return lax.dynamic_slice_in_dim(vector, lax.axis_index("fsdp") * width, width)


def shards(
    inputs,
    classes,
    offset_table,
    bias_table,
    qkv_weight,
    qkv_gain,
    qkv_shift,
    out_weight,
    out_gain,
    out_shift,
    up_weight,
    up_gain,
    up_shift,
    down_weight,
    down_gain,
    down_shift,
    cotangent,
):
    gathered = (
        lax.all_gather(qkv_weight, "fsdp", axis=0, tiled=True),
        lax.all_gather(qkv_gain, "fsdp", axis=0, tiled=True),
        lax.all_gather(qkv_shift, "fsdp", axis=0, tiled=True),
        lax.all_gather(out_weight, "fsdp", axis=0, tiled=True),
        lax.all_gather(out_gain, "fsdp", axis=0, tiled=True),
        lax.all_gather(out_shift, "fsdp", axis=0, tiled=True),
        lax.all_gather(up_weight, "fsdp", axis=0, tiled=True),
        lax.all_gather(up_gain, "fsdp", axis=0, tiled=True),
        lax.all_gather(up_shift, "fsdp", axis=0, tiled=True),
        lax.all_gather(down_weight, "fsdp", axis=0, tiled=True),
        lax.all_gather(down_gain, "fsdp", axis=0, tiled=True),
        lax.all_gather(down_shift, "fsdp", axis=0, tiled=True),
    )
    qkv_full, qkv_gains, qkv_shifts, out_full, out_gains, out_shifts = gathered[:6]
    images = inputs.shape[0]
    length = images * SLOT
    limits = jnp.where(
        classes == 0,
        (GRID - 8) * (GRID - 8),
        jnp.where(classes == 1, (GRID - 4) * (GRID - 4), SLOT),
    )
    keep = (jnp.arange(SLOT)[None, :] < limits[:, None]).astype(jnp.float32)
    weights = keep.reshape(-1, 1)
    flat = inputs.reshape(length, -1)
    z_qkv = jnp.dot(flat, qkv_full, preferred_element_type=jnp.float32)
    mixed_f, hat_qkv, scale_qkv, total = norm_forward(z_qkv, weights, qkv_gains, qkv_shifts)
    mixed = mixed_f.astype(jnp.bfloat16).reshape(images, SLOT, HEADS, -1)
    query = mixed[..., :KEY]
    keys = mixed[..., KEY : 2 * KEY]
    values = mixed[..., 2 * KEY :]
    class_onehot = (classes[:, None] == jnp.arange(CLASSES)[None, :]).astype(jnp.float32)
    class_bias = bias_table[:, offset_table]
    bias = jnp.einsum("ic,hcqp->ihqp", class_onehot, class_bias, precision=lax.Precision.HIGHEST)
    scores = attention_scores(query, keys, bias, keep)
    top = jnp.max(scores, axis=-1, keepdims=True)
    expo = jnp.exp(scores - top)
    denom = jnp.sum(expo, axis=-1, keepdims=True)
    probs = (expo / denom).astype(jnp.bfloat16)
    log_total = top + jnp.log(denom)
    attended = jnp.einsum(
        "ihqp,iphv->iqhv", probs, values, preferred_element_type=jnp.float32
    ).reshape(length, -1)
    activated = jax.nn.silu(attended).astype(jnp.bfloat16)
    z_out = jnp.dot(activated, out_full, preferred_element_type=jnp.float32)
    branch, hat_out, scale_out, unused_out = norm_forward(z_out, weights, out_gains, out_shifts)
    middle = flat.astype(jnp.float32) + branch
    middle_low = middle.astype(jnp.bfloat16)
    second = gathered[6:]
    up_full, up_gains, up_shifts, down_full, down_gains, down_shifts = second
    z_up = jnp.dot(middle_low, up_full, preferred_element_type=jnp.float32)
    up_normed, hat_up, scale_up, unused_up = norm_forward(z_up, weights, up_gains, up_shifts)
    hidden = jax.nn.silu(up_normed).astype(jnp.bfloat16)
    z_down = jnp.dot(hidden, down_full, preferred_element_type=jnp.float32)
    down_normed, hat_down, scale_down, unused_down = norm_forward(
        z_down, weights, down_gains, down_shifts
    )
    output = ((middle + down_normed) * weights).astype(jnp.bfloat16).reshape(inputs.shape)
    grad_out = cotangent.astype(jnp.float32).reshape(length, -1) * weights
    dz_down, down_gain_grad, down_shift_grad = norm_backward(
        grad_out, hat_down, scale_down, total, down_gains, weights
    )
    dz_down_low = dz_down.astype(jnp.bfloat16)
    down_grad = left_product(hidden, dz_down_low)
    grad_up = right_product(dz_down_low, down_full) * silu_slope(up_normed)
    dz_up, up_gain_grad, up_shift_grad = norm_backward(
        grad_up, hat_up, scale_up, total, up_gains, weights
    )
    dz_up_low = dz_up.astype(jnp.bfloat16)
    up_grad = left_product(middle_low, dz_up_low)
    grad_middle = grad_out + right_product(dz_up_low, up_full)
    dz_out, out_gain_grad, out_shift_grad = norm_backward(
        grad_middle, hat_out, scale_out, total, out_gains, weights
    )
    dz_out_low = dz_out.astype(jnp.bfloat16)
    out_grad = left_product(activated, dz_out_low)
    grad_att = (right_product(dz_out_low, out_full) * silu_slope(attended)).astype(jnp.bfloat16)
    grad_att = grad_att.reshape(images, SLOT, HEADS, VALD)
    again = attention_scores(query, keys, bias, keep)
    prob_full = jnp.exp(again - log_total)
    prob_low = prob_full.astype(jnp.bfloat16)
    dprob = jnp.einsum("iqhv,iphv->ihqp", grad_att, values, preferred_element_type=jnp.float32)
    grad_values = jnp.einsum(
        "ihqp,iqhv->iphv", prob_low, grad_att, preferred_element_type=jnp.float32
    )
    dscore = prob_full * (dprob - jnp.sum(dprob * prob_full, axis=-1, keepdims=True))
    per_class = jnp.einsum("ic,ihqp->cqph", class_onehot, dscore, precision=lax.Precision.HIGHEST)
    local_table = jax.ops.segment_sum(
        per_class.reshape(-1, HEADS), offset_table.reshape(-1), num_segments=NOFF
    ).T
    score_low = dscore.astype(jnp.bfloat16)
    grad_query = jnp.einsum(
        "ihqp,iphk->iqhk", score_low, keys, preferred_element_type=jnp.float32
    ) * KEY ** (-0.5)
    grad_keys = jnp.einsum(
        "ihqp,iqhk->iphk", score_low, query, preferred_element_type=jnp.float32
    ) * KEY ** (-0.5)
    grad_mixed = jnp.concatenate([grad_query, grad_keys, grad_values], axis=-1).reshape(length, -1)
    dz_qkv, qkv_gain_grad, qkv_shift_grad = norm_backward(
        grad_mixed, hat_qkv, scale_qkv, total, qkv_gains, weights
    )
    dz_qkv_low = dz_qkv.astype(jnp.bfloat16)
    qkv_grad = left_product(flat, dz_qkv_low)
    input_grad = (grad_middle + right_product(dz_qkv_low, qkv_full)).reshape(inputs.shape)
    table_grad = lax.psum(local_table, ("dp", "fsdp"))
    whole = (
        lax.psum(qkv_grad.astype(jnp.bfloat16), "dp").astype(jnp.float32),
        lax.psum(out_grad.astype(jnp.bfloat16), "dp").astype(jnp.float32),
        lax.psum(up_grad.astype(jnp.bfloat16), "dp").astype(jnp.float32),
        lax.psum(down_grad.astype(jnp.bfloat16), "dp").astype(jnp.float32),
    )
    summed = (
        lax.psum_scatter(
            whole[0].astype(jnp.bfloat16), "fsdp", scatter_dimension=0, tiled=True
        ).astype(jnp.float32),
        lax.psum_scatter(
            whole[1].astype(jnp.bfloat16), "fsdp", scatter_dimension=0, tiled=True
        ).astype(jnp.float32),
        lax.psum_scatter(
            whole[2].astype(jnp.bfloat16), "fsdp", scatter_dimension=0, tiled=True
        ).astype(jnp.float32),
        lax.psum_scatter(
            whole[3].astype(jnp.bfloat16), "fsdp", scatter_dimension=0, tiled=True
        ).astype(jnp.float32),
    )
    return (
        output,
        input_grad,
        table_grad,
        summed[0],
        own_slice(qkv_gain_grad),
        own_slice(qkv_shift_grad),
        summed[1],
        own_slice(out_gain_grad),
        own_slice(out_shift_grad),
        summed[2],
        own_slice(up_gain_grad),
        own_slice(up_shift_grad),
        summed[3],
        own_slice(down_gain_grad),
        own_slice(down_shift_grad),
    )


def solution(mesh):
    placed = (
        P(("dp", "fsdp"), None, None),
        P(("dp", "fsdp")),
        P(),
        P(),
        P("fsdp", None),
        P("fsdp"),
        P("fsdp"),
        P("fsdp", None),
        P("fsdp"),
        P("fsdp"),
        P("fsdp", None),
        P("fsdp"),
        P("fsdp"),
        P("fsdp", None),
        P("fsdp"),
        P("fsdp"),
        P(("dp", "fsdp"), None, None),
    )
    return jax.shard_map(
        shards,
        mesh=mesh,
        in_specs=placed,
        out_specs=(
            P(("dp", "fsdp"), None, None),
            P(("dp", "fsdp"), None, None),
            P(),
            P("fsdp", None),
            P("fsdp"),
            P("fsdp"),
            P("fsdp", None),
            P("fsdp"),
            P("fsdp"),
            P("fsdp", None),
            P("fsdp"),
            P("fsdp"),
            P("fsdp", None),
            P("fsdp"),
            P("fsdp"),
        ),
        check_vma=False,
    )
```

profile of v0, /device:TPU:0, one launch (start us, length us, event | category | flops | bytes accessed | tf_op | source)
XLA Modules:
  0.0 3830.3 jit_solution(13546214082741459235)
XLA Ops:
  18.2 23.3 all-reduce.16
  41.6 31.0 all_gather.36
  81.1 37.1 all-reduce.15
  151.1 32.8 all_gather.39
  183.9 30.7 all_gather.42
  214.6 32.7 all_gather.45
  257.0 631.7 %gather_fusion = f32[314928,4]{1,0:T(8,128)} fusion(f32[4,324]{0,1:T(8,128)S(1)} %copy.87, s32[315392]{0:T(1024)} %pad_clamp_fusion), kind=kCustom, calls=%fused_computation | custom fusion | bytes 11337408 | tf_op jit(solution)/shard_map/gather | solution.py:119
  888.7 80.6 %copy.88 = f32[314928,4]{0,1:T(4,128)} copy(f32[314928,4]{1,0:T(8,128)} %gather_fusion) | data formatting | bytes 10077696 | tf_op jit(solution)/shard_map/gather | solution.py:119
  980.0 15.5 fusion.6
  995.5 17.0 copy.90
  1012.5 16.2 fusion.51
  1037.1 11.7 fusion.20
  1057.5 39.6 %all-reduce.14 = (f32[256]{0:T(256)S(1)}, f32[256]{0:T(256)S(1)}) all-reduce(f32[256]{0:T(256)S(1)} %get-tuple-element.69, f32[256]{0:T(256)S(1)} %get-tuple-element.68), channel_id=1, replica_groups=mesh['dp'=4,'fsdp'=8] {'dp','fsdp'}, use_global_device_ids=true, to_apply=%region_9.10 | all-reduce | flops 512 | bytes 4096 | tf_op jit(solution)/shard_map/psum | solution.py:24
  1103.5 40.8 %all-reduce.13 = (f32[512]{0:T(512)S(1)}, f32[512]{0:T(512)S(1)}) all-reduce(f32[512]{0:T(512)S(1)} %get-tuple-element.63, f32[512]{0:T(512)S(1)} %get-tuple-element.62), channel_id=1, replica_groups=mesh['dp'=4,'fsdp'=8] {'dp','fsdp'}, use_global_device_ids=true, to_apply=%region_15.16 | all-reduce | flops 1024 | bytes 8192 | tf_op jit(solution)/shard_map/psum | solution.py:24
  1151.6 39.1 %all-reduce.12 = (f32[256]{0:T(256)S(1)}, f32[256]{0:T(256)S(1)}) all-reduce(f32[256]{0:T(256)S(1)} %get-tuple-element.67, f32[256]{0:T(256)S(1)} %get-tuple-element.66), channel_id=1, replica_groups=mesh['dp'=4,'fsdp'=8] {'dp','fsdp'}, use_global_device_ids=true, to_apply=%region_17.18 | all-reduce | flops 512 | bytes 4096 | tf_op jit(solution)/shard_map/psum | solution.py:24
  1193.7 40.8 %all-reduce.11 = (f32[256]{0:T(256)S(1)}, f32[256]{0:T(256)S(1)}) all-reduce(f32[256]{0:T(256)S(1)} %multiply_reduce_fusion.8, f32[256]{0:T(256)S(1)} %multiply_reduce_fusion.9), channel_id=1, replica_groups=mesh['dp'=4,'fsdp'=8] {'dp','fsdp'}, use_global_device_ids=true, to_apply=%region_23.24 | all-reduce | flops 512 | bytes 4096 | tf_op jit(solution)/shard_map/psum | solution.py:41
  1244.9 39.2 %all-reduce.10 = (f32[512]{0:T(512)S(1)}, f32[512]{0:T(512)S(1)}) all-reduce(f32[512]{0:T(512)S(1)} %get-tuple-element.65, f32[512]{0:T(512)S(1)} %get-tuple-element.64), channel_id=1, replica_groups=mesh['dp'=4,'fsdp'=8] {'dp','fsdp'}, use_global_device_ids=true, to_apply=%region_27.28 | all-reduce | flops 1024 | bytes 8192 | tf_op jit(solution)/shard_map/psum | solution.py:41
  1293.3 41.2 %all-reduce.9 = (f32[256]{0:T(256)S(1)}, f32[256]{0:T(256)S(1)}) all-reduce(f32[256]{0:T(256)S(1)} %get-tuple-element.71, f32[256]{0:T(256)S(1)} %get-tuple-element.70), channel_id=1, replica_groups=mesh['dp'=4,'fsdp'=8] {'dp','fsdp'}, use_global_device_ids=true, to_apply=%region_31.32 | all-reduce | flops 512 | bytes 4096 | tf_op jit(solution)/shard_map/psum | solution.py:41
  1351.4 11.1 fusion.21
  1373.2 11.4 subtract_multiply_fusion
  1393.4 16.5 copy.104
  1440.1 13.4 fusion.49
  1453.7 13.3 copy.117
  1466.9 12.2 reshape.208
  1485.8 70.2 %copy.106 = f32[314928,4]{1,0:T(8,128)} copy(f32[314928,4]{0,1:T(4,128)} %reshape.158) | data formatting | bytes 10077696 | tf_op jit(solution)/shard_map/reshape | solution.py:175
  1556.0 1921.0 %scatter_custom_fusion = f32[324,4]{1,0:T(8,128)S(1)} fusion(s32[314928]{0:T(1024)} %reshape.156, f32[314928,4]{1,0:T(8,128)} %copy.106, f32[]{:T(128)} %constant.23.clone.1), kind=kCustom, calls=%fused_computation.81 | custom fusion | flops 1259712 | bytes 5696 | tf_op jit(solution)/shard_map/scatter-add | solution.py:174
  3477.0 42.3 %all-reduce.8 = (f32[768]{0:T(1024)S(1)}, f32[768]{0:T(1024)S(1)}, f32[4,324]{0,1:T(8,128)S(1)}) all-reduce(f32[768]{0:T(1024)S(1)} %multiply_reduce_fusion.1, f32[768]{0:T(1024)S(1)} %reduce_sum.203, f32[4,324]{0,1:T(8,128)S(1)} %bitcast.94), channel_id=1, replica_groups=mesh['dp'=4,'fsdp'=8] {'dp','fsdp'}, use_global_device_ids=true, to_apply=%region_36.37 | all-reduce | flops 2832 | bytes 22656 | tf_op jit(solution)/shard_map/psum | solution.py:41
  3542.4 49.8 %reduce-scatter.13.cloned.1.call-done = bf16[32,768]{1,0:T(8,128)(2,1)} async-done(((bf16[256,768]{1,0:T(8,128)(2,1)}), bf16[32,768]{1,0:T(8,128)(2,1)}) %reduce-scatter.13.cloned.1.call-update) | async-done | bytes 49168
  3593.9 62.0 %reduce-scatter.11.cloned.1.call-done = bf16[64,256]{1,0:T(8,128)(2,1)} async-done(((bf16[512,256]{1,0:T(8,128)(2,1)}), bf16[64,256]{1,0:T(8,128)(2,1)}) %reduce-scatter.11.cloned.1.call-update) | async-done | bytes 32784 | tf_op jit(solution)/shard_map/reduce_scatter | solution.py:208
  3655.9 64.2 %reduce-scatter.7.cloned.1.call-done = bf16[64,256]{1,0:T(8,128)(2,1)} async-done(((bf16[512,256]{1,0:T(8,128)(2,1)}), bf16[64,256]{1,0:T(8,128)(2,1)}) %reduce-scatter.7.cloned.1.call-update) | async-done | bytes 32784 | tf_op jit(solution)/shard_map/reduce_scatter | solution.py:202
  3720.0 63.5 %reduce-scatter.9.cloned.1.call-done = bf16[32,512]{1,0:T(8,128)(2,1)} async-done(((bf16[256,512]{1,0:T(8,128)(2,1)}), bf16[32,512]{1,0:T(8,128)(2,1)}) %reduce-scatter.9.cloned.1.call-update) | async-done | bytes 32784 | tf_op jit(solution)/shard_map/reduce_scatter | solution.py:205
  3805.9 11.5 all-reduce.20.cloned.1.call-done
  (236 shorter events, 250.0 us)
Async XLA Ops:
  7.2 9.1 copy-start.52
  7.2 9.3 copy-start.53
  7.2 9.5 copy-start.54
  7.2 9.8 copy-start.55
  7.2 10.0 copy-start.56
  7.3 10.3 copy-start.57
  7.3 10.5 copy-start.58
  7.3 10.7 copy-start.59
  7.3 34.3 copy-start.33
  7.3 3585.0 %reduce-scatter.13.cloned.1.call-start = ((), (), s32[]{:S(2)}) async-start(), calls=%async_computation.7 | async-start | bytes 442368
  41.6 77.3 %copy-start.34 = (f32[768]{0:T(1024)}, f32[768]{0:T(1024)S(1)}, u32[]{:S(2)}) copy-start(f32[768]{0:T(1024)S(1)} %convert_element_type.131) | copy-start | bytes 9220
  148.0 35.8 copy-start.37
  148.1 66.5 %copy-start.38 = (bf16[64,256]{1,0:T(8,128)(2,1)S(1)}, bf16[64,256]{1,0:T(8,128)(2,1)}, u32[]{:S(2)}) copy-start(bf16[64,256]{1,0:T(8,128)(2,1)} %param.30) | copy-start | bytes 98308
  969.3 10.8 copy-start.40
  1234.5 10.3 copy-start.43
  1234.5 10.3 copy-start.45
  1290.6 43.8 %copy-start.51 = (f32[256]{0:T(256)S(1)}, f32[256]{0:T(256)}, u32[]{:S(2)}) copy-start(f32[256]{0:T(256)} %convert_element_type.143) | copy-start | bytes 3076
  1351.4 11.1 copy-start.9
  1373.2 11.5 copy-start.15
  1423.8 8.7 copy-start.16
  1466.9 12.2 copy-start.30
  1466.9 12.2 copy-start.32
  1485.8 2033.5 %copy-start.35 = (f32[768]{0:T(1024)S(1)}, f32[768]{0:T(1024)}, u32[]{:S(2)}) copy-start(f32[768]{0:T(1024)} %copy-done.34) | copy-start | bytes 9220
  3519.3 9.8 copy-start.5
  3531.4 124.4 %reduce-scatter.11.cloned.1.call-start = ((), (), s32[]{:S(2)}) async-start(), calls=%async_computation.6 | async-start | bytes 294912 | tf_op jit(solution)/shard_map/reduce_scatter | solution.py:208
  3534.5 185.6 %reduce-scatter.7.cloned.1.call-start = ((), (), s32[]{:S(2)}) async-start(), calls=%async_computation.4 | async-start | bytes 294912 | tf_op jit(solution)/shard_map/reduce_scatter | solution.py:202
  3538.3 245.2 %copy-start.2 = (f32[2592,256]{1,0:T(8,128)S(1)}, f32[2592,256]{1,0:T(8,128)}, u32[]{:S(2)}) copy-start(f32[2592,256]{1,0:T(8,128)} %get-tuple-element.125) | copy-start | bytes 7962628
  3538.3 245.2 %copy-start.22 = (bf16[256,768]{1,0:T(8,128)(2,1)S(1)}, bf16[256,768]{1,0:T(8,128)(2,1)}, u32[]{:S(2)}) copy-start(bf16[256,768]{1,0:T(8,128)(2,1)} %copy-done.21) | copy-start | bytes 1179652
  3538.4 245.2 %reduce-scatter.9.cloned.1.call-start = ((), (), s32[]{:S(2)}) async-start(), calls=%async_computation.5 | async-start | bytes 294912 | tf_op jit(solution)/shard_map/reduce_scatter | solution.py:205
  3542.4 275.0 %all-reduce.20.cloned.1.call-start = ((), (), s32[]{:S(2)}) async-start(), calls=%async_computation.8 | async-start | bytes 589824 | tf_op jit(solution)/shard_map/psum | solution.py:193
  3783.6 9.2 copy-start.48
  3788.5 11.7 copy-start.7
  (34 other events, 164.6 us)
Sparse Core Ops, SparseCore 0:
  3531.5 60.6 reduce-scatter.12
  3595.6 60.2 reduce-scatter.10
  3659.8 60.2 reduce-scatter.6
  3723.2 60.2 reduce-scatter.8
  3785.9 31.5 all-reduce.19
where the time goes:
time: 3870 us; the launch traced here: 3830 us
  other arithmetic  2010 us (52%)
  local copies, waits for them, and re-layouts  954 us (25%)
  blocking collectives  471 us (12%)
  waiting for transfers between devices  251 us (6%)
  matrix products  125 us (3%)
    scatter-add x1, other arithmetic, shards(): jax.ops.segment_sum(per_class.reshape(-1, HEADS), offset_table.reshape(-1...  1920 us
    gather x3, local copies, waits for them, and re-layouts, shards(): class_bias = bias_table[:, offset_table]  723 us
    psum x4, blocking collectives, norm_backward(): lax.psum((jnp.sum(grad, axis=0), jnp.sum(grad * normed, axis=0)), ('dp',...  163 us
    psum x4, blocking collectives, norm_forward(): lax.psum((jnp.sum(value * weights, axis=0), jnp.sum(value * value * weigh...  157 us
    reshape x2, local copies, waits for them, and re-layouts, shards(): per_class.reshape(-1, HEADS)  78.9 us
  transfers between devices with their start and end apart: 5, of which 5 were waited for; matrix products, arithmetic and copies ran while one was open for 1% of the time, Pallas kernels for 0%

commit v1 on v0

--- a/solution.py
+++ b/solution.py
@@ -1,6 +1,8 @@
 import jax
 import jax.numpy as jnp
 from jax import lax
+from jax.experimental import pallas as pl
+from jax.experimental.pallas import tpu as pltpu
 from jax.sharding import PartitionSpec as P
 
 HEADS = 4
@@ -13,6 +15,303 @@
 
 
 EPS = 1e-05
+LOG2E = 1.4426950408889634
+LN2 = 0.6931471805599453
+ROWS = 336
+PARTS = ((10, 100, 112, 128), (14, 196, 208, 256), (18, 324, 336, 384))
+VMEM = pl.BlockSpec(memory_space=pltpu.VMEM)
+
+
+def dot_nn(left, right):
+    return jnp.dot(left, right, preferred_element_type=jnp.float32)
+
+
+def dot_nt(left, right):
+    return lax.dot_general(left, right, (((1,), (1,)), ((), ())), preferred_element_type=jnp.float32)
+
+
+def dot_tn(left, right):
+    return lax.dot_general(left, right, (((0,), (0,)), ((), ())), preferred_element_type=jnp.float32)
+
+
+def pad_rows(value, rows):
+    if value.shape[0] == rows:
+        return value
+    return jnp.concatenate([value, jnp.zeros((rows - value.shape[0], value.shape[1]), value.dtype)], axis=0)
+
+
+def pad_lanes(value, lanes):
+    if value.shape[1] == lanes:
+        return value
+    return jnp.concatenate([value, jnp.zeros((value.shape[0], lanes - value.shape[1]), value.dtype)], axis=1)
+
+
+def bias_tables(off_ref, table_ref, index_ref, outs):
+    tables = []
+    for head in range(HEADS):
+        row = pad_lanes(table_ref[head : head + 1, :], 384) * LOG2E
+        tables.append([jnp.broadcast_to(row[:, 128 * k : 128 * k + 128], (8, 128)) for k in range(3)])
+    index_ref[...] = jnp.zeros_like(index_ref)
+    for number, (_, amount, rows, lanes) in enumerate(PARTS):
+        index_ref[:SLOT, :SLOT] = off_ref[number]
+
+        def tile(step, _, amount=amount, lanes=lanes, out=outs[number]):
+            at = pl.multiple_of(step * 8, 8)
+            for block in range(lanes // 128):
+                index = index_ref[pl.ds(at, 8), 128 * block : 128 * block + 128]
+                low = index & 127
+                part = index >> 7
+                valid = lax.broadcasted_iota(jnp.int32, (8, 128), 1) + 128 * block < amount
+                for head in range(HEADS):
+                    found = [
+                        jnp.take_along_axis(tables[head][k], low, axis=1, mode="promise_in_bounds")
+                        for k in range(3)
+                    ]
+                    value = jnp.where(part == 0, found[0], jnp.where(part == 1, found[1], found[2]))
+                    column = (head % 2) * lanes + 128 * block
+                    out[head // 2, pl.ds(at, 8), column : column + 128] = jnp.where(valid, value, -1e30)
+            return 0
+
+        lax.fori_loop(0, rows // 8, tile, 0)
+
+
+def head_keys(keys, pair, lanes):
+    owner = lax.broadcasted_iota(jnp.int32, keys.shape, 1) // KEY
+    zero = jnp.zeros_like(keys)
+    return jnp.concatenate(
+        [pad_rows(jnp.where(owner == 2 * pair + side, keys, zero), lanes) for side in range(2)], axis=0
+    )
+
+
+def pair_values(values, lanes):
+    zero = jnp.zeros((lanes, VALD), values.dtype)
+    top = jnp.concatenate([pad_rows(values[:, :VALD], lanes), zero], axis=1)
+    low = jnp.concatenate([zero, pad_rows(values[:, VALD:], lanes)], axis=1)
+    return jnp.concatenate([top, low], axis=0)
+
+
+def attend_kernel(class_ref, mixed_ref, bias0, bias1, bias2, att_ref, p_ref, r_ref):
+    kind = class_ref[pl.program_id(0)]
+    for number, (_, amount, rows, lanes) in enumerate(PARTS):
+
+        @pl.when(kind == number)
+        def _(amount=amount, rows=rows, lanes=lanes, bias=(bias0, bias1, bias2)[number]):
+            query = mixed_ref[0, :rows, :128]
+            keys = mixed_ref[0, :rows, 128:256]
+            kept = lax.broadcasted_iota(jnp.int32, (rows, VALD), 0) < amount
+            lane = lax.broadcasted_iota(jnp.int32, (rows, 128), 1)
+            shares = jnp.zeros((rows, 128), jnp.float32)
+            for pair in range(2):
+                scores = dot_nt(query, head_keys(keys, pair, lanes)) + bias[pair]
+                parts, inverse = [], []
+                for side in range(2):
+                    own = scores[:, side * lanes : (side + 1) * lanes]
+                    expo = jnp.exp2(own - jnp.max(own, axis=1, keepdims=True))
+                    share = 1.0 / jnp.sum(expo, axis=1, keepdims=True)
+                    shares = jnp.where(lane == 2 * pair + side, share, shares)
+                    parts.append(expo.astype(jnp.bfloat16))
+                    inverse.append(share)
+                both = jnp.concatenate(parts, axis=1)
+                p_ref[0, :rows, 2 * pair * lanes : 2 * (pair + 1) * lanes] = both
+                values = mixed_ref[0, :rows, 256 + 256 * pair : 512 + 256 * pair]
+                sums = dot_nn(both, pair_values(values, lanes))
+                for side in range(2):
+                    own = sums[:, side * VALD : (side + 1) * VALD] * inverse[side]
+                    at = (2 * pair + side) * VALD
+                    att_ref[0, :rows, at : at + VALD] = jnp.where(kept, own, 0.0).astype(jnp.bfloat16)
+            r_ref[0, :rows, :] = shares
+            if rows < ROWS:
+                att_ref[0, rows:, :] = jnp.zeros((ROWS - rows, att_ref.shape[2]), jnp.bfloat16)
+
+
+def back_kernel(class_ref, mixed_ref, p_ref, r_ref, g_ref, att_ref, gmix_ref, acc0, acc1, acc2):
+    accs = (acc0, acc1, acc2)
+
+    @pl.when(pl.program_id(0) == 0)
+    def _():
+        for acc in accs:
+            acc[...] = jnp.zeros_like(acc)
+
+    kind = class_ref[pl.program_id(0)]
+    for number, (_, amount, rows, lanes) in enumerate(PARTS):
+
+        @pl.when(kind == number)
+        def _(rows=rows, lanes=lanes, acc=accs[number]):
+            query = mixed_ref[0, :rows, :128]
+            keys = mixed_ref[0, :rows, 128:256]
+            owner = lax.broadcasted_iota(jnp.int32, (rows, 128), 1) // KEY
+            d_query = jnp.zeros((rows, 128), jnp.float32)
+            d_keys = jnp.zeros((rows, 128), jnp.float32)
+            for pair in range(2):
+                grads, deltas = [], []
+                for side in range(2):
+                    head = 2 * pair + side
+                    at = head * VALD
+                    grad = g_ref[0, :rows, at : at + VALD].astype(jnp.float32) * r_ref[0, :rows, head : head + 1]
+                    own = att_ref[0, :rows, at : at + VALD].astype(jnp.float32)
+                    deltas.append(jnp.sum(grad * own, axis=1, keepdims=True))
+                    grads.append(grad.astype(jnp.bfloat16))
+                both = jnp.concatenate(grads, axis=1)
+                values = mixed_ref[0, :rows, 256 + 256 * pair : 512 + 256 * pair]
+                d_probs = dot_nt(both, pair_values(values, lanes))
+                probs = p_ref[0, :rows, 2 * pair * lanes : 2 * (pair + 1) * lanes]
+                low = []
+                for side in range(2):
+                    cut = slice(side * lanes, (side + 1) * lanes)
+                    d_score = probs[:, cut].astype(jnp.float32) * (d_probs[:, cut] - deltas[side])
+                    acc[pair, :, cut] += d_score
+                    low.append(d_score.astype(jnp.bfloat16))
+                d_low = jnp.concatenate(low, axis=1)
+                d_query = d_query + dot_nn(d_low, head_keys(keys, pair, lanes))
+                turned = dot_tn(d_low, query)
+                d_values = dot_tn(probs, both)
+                for side in range(2):
+                    head = 2 * pair + side
+                    d_keys = jnp.where(owner == head, turned[side * lanes : side * lanes + rows], d_keys)
+                    at = 256 + head * VALD
+                    gmix_ref[0, :rows, at : at + VALD] = d_values[
+                        side * lanes : side * lanes + rows, side * VALD : (side + 1) * VALD
+                    ].astype(jnp.bfloat16)
+            gmix_ref[0, :rows, :128] = (d_query * KEY ** (-0.5)).astype(jnp.bfloat16)
+            gmix_ref[0, :rows, 128:256] = (d_keys * LN2).astype(jnp.bfloat16)
+            if rows < ROWS:
+                gmix_ref[0, rows:, :] = jnp.zeros((ROWS - rows, gmix_ref.shape[2]), jnp.bfloat16)
+
+
+def table_sums(off_ref, accs):
+    totals = [jnp.zeros((24, 640), jnp.float32) for _ in range(HEADS)]
+    for number, (side_of, amount, rows, lanes) in enumerate(PARTS):
+        offsets = off_ref[number]
+        row = lax.broadcasted_iota(jnp.int32, (SLOT, 1), 0)
+        most = jnp.max(offsets, axis=1, keepdims=True)
+        corner = jnp.min(jnp.where(most == (side_of - 1) * (GRID + 1), row, SLOT), axis=0, keepdims=True)
+        place = jnp.sum(jnp.where(row == corner, offsets, 0), axis=0, keepdims=True)
+        place = jnp.where(lax.broadcasted_iota(jnp.int32, (1, SLOT), 1) < amount, place, -1)
+        wide = jnp.concatenate([place, jnp.full((1, 384 - SLOT), -1, jnp.int32)], axis=1)
+        cell = lax.broadcasted_iota(jnp.int32, (24 * side_of, 1), 0)
+        cell_row = (cell * 2731) >> 16
+        cell_col = cell - 24 * cell_row
+        code = jnp.where(cell_col < side_of, cell_row * GRID + cell_col, -2)
+        left = (code == wide[:, :rows]).astype(jnp.float32).astype(jnp.bfloat16)
+        spot = lax.broadcasted_iota(jnp.int32, (384, 1), 0)
+        right = (spot == wide[:, :lanes]).astype(jnp.float32).astype(jnp.bfloat16)
+        for head in range(HEADS):
+            at = (head % 2) * lanes
+            score = accs[number][head // 2, :, at : at + lanes].astype(jnp.bfloat16)
+            sorted_rows = dot_nn(left, score).astype(jnp.bfloat16)
+            both = dot_nt(sorted_rows, right)
+            for line in range(side_of):
+                part = pad_lanes(both[24 * line : 24 * line + 24], 640)
+                totals[head] = totals[head] + pltpu.roll(part, (GRID - 1 - line) * GRID, 1)
+    lane = lax.broadcasted_iota(jnp.int32, (24, 640), 1)
+    lane_row = (lane * 3641) >> 16
+    away = jnp.abs(lane - GRID * lane_row - lax.broadcasted_iota(jnp.int32, (24, 640), 0))
+    wide_row = lax.broadcasted_iota(jnp.int32, (640, 1), 0)
+    wide_row = jnp.abs(((wide_row * 3641) >> 16) - (GRID - 1))
+    out_lane = lax.broadcasted_iota(jnp.int32, (1, 384), 1)
+    out_row = (out_lane * 3641) >> 16
+    fold = (wide_row == out_row).astype(jnp.float32).astype(jnp.bfloat16)
+    out_col = out_lane - GRID * out_row
+    pick = lax.broadcasted_iota(jnp.int32, (24, 1), 0) == out_col
+    rows_out = []
+    for head in range(HEADS):
+        lines = [
+            jnp.sum(jnp.where(away == d, totals[head], 0.0), axis=0, keepdims=True) for d in range(GRID)
+        ]
+        lines = pad_rows(jnp.concatenate(lines, axis=0), 24)
+        high = lines.astype(jnp.bfloat16)
+        low = (lines - high.astype(jnp.float32)).astype(jnp.bfloat16)
+        spread = dot_nn(high, fold) + dot_nn(low, fold)
+        rows_out.append(jnp.sum(jnp.where(pick, spread, 0.0), axis=0, keepdims=True))
+    return jnp.concatenate(rows_out, axis=0)
+
+
+def bias_kernel(off_ref, table_ref, out0, out1, out2, index_ref):
+    bias_tables(off_ref, table_ref, index_ref, (out0, out1, out2))
+
+
+def bias_call(offset_table, bias_table):
+    return pl.pallas_call(
+        bias_kernel,
+        out_shape=[jax.ShapeDtypeStruct((2, r, 2 * l), jnp.float32) for _, _, r, l in PARTS],
+        in_specs=[VMEM, VMEM],
+        out_specs=[VMEM] * 3,
+        scratch_shapes=[pltpu.VMEM((ROWS, 384), jnp.int32)],
+        compiler_params=pltpu.CompilerParams(vmem_limit_bytes=48 * 2**20),
+    )(offset_table, bias_table)
+
+
+def image_spec(width):
+    return pl.BlockSpec((1, ROWS, width), lambda i, c: (i, 0, 0))
+
+
+def whole_spec(shape):
+    return pl.BlockSpec(shape, lambda i, c: (0,) * len(shape))
+
+
+def attend_call(classes, mixed, biases):
+    images = mixed.shape[0]
+    return pl.pallas_call(
+        attend_kernel,
+        grid_spec=pltpu.PrefetchScalarGridSpec(
+            num_scalar_prefetch=1,
+            grid=(images,),
+            in_specs=[image_spec(768)] + [whole_spec(b.shape) for b in biases],
+            out_specs=[image_spec(512), image_spec(1536), image_spec(128)],
+        ),
+        out_shape=[
+            jax.ShapeDtypeStruct((images, ROWS, 512), jnp.bfloat16),
+            jax.ShapeDtypeStruct((images, ROWS, 1536), jnp.bfloat16),
+            jax.ShapeDtypeStruct((images, ROWS, 128), jnp.float32),
+        ],
+        compiler_params=pltpu.CompilerParams(vmem_limit_bytes=48 * 2**20),
+    )(classes, mixed, *biases)
+
+
+def back_call(classes, mixed, probs, shares, grad, attended):
+    images = mixed.shape[0]
+    shapes = [(2, r, 2 * l) for _, _, r, l in PARTS]
+    return pl.pallas_call(
+        back_kernel,
+        grid_spec=pltpu.PrefetchScalarGridSpec(
+            num_scalar_prefetch=1,
+            grid=(images,),
+            in_specs=[image_spec(768), image_spec(1536), image_spec(128), image_spec(512), image_spec(512)],
+            out_specs=[image_spec(768)] + [whole_spec(s) for s in shapes],
+        ),
+        out_shape=[jax.ShapeDtypeStruct((images, ROWS, 768), jnp.bfloat16)]
+        + [jax.ShapeDtypeStruct(s, jnp.float32) for s in shapes],
+        compiler_params=pltpu.CompilerParams(vmem_limit_bytes=48 * 2**20),
+    )(classes, mixed, probs, shares, grad, attended)
+
+
+def table_kernel(off_ref, acc0, acc1, acc2, out_ref):
+    out_ref[...] = table_sums(off_ref, (acc0, acc1, acc2))
+
+
+def table_call(offset_table, accs):
+    return pl.pallas_call(
+        table_kernel,
+        out_shape=jax.ShapeDtypeStruct((HEADS, 384), jnp.float32),
+        in_specs=[VMEM] * 4,
+        out_specs=VMEM,
+        compiler_params=pltpu.CompilerParams(vmem_limit_bytes=48 * 2**20),
+    )(offset_table, *accs)
+
+
+def arrange(columns):
+    lead = columns.shape[:-1]
+    heads = columns.reshape(lead + (HEADS, 2 * KEY + VALD))
+    parts = (heads[..., :KEY], heads[..., KEY : 2 * KEY], heads[..., 2 * KEY :])
+    return jnp.concatenate([part.reshape(lead + (-1,)) for part in parts], axis=-1)
+
+
+def restore(columns):
+    lead = columns.shape[:-1]
+    query = columns[..., :128].reshape(lead + (HEADS, KEY))
+    keys = columns[..., 128:256].reshape(lead + (HEADS, KEY))
+    values = columns[..., 256:].reshape(lead + (HEADS, VALD))
+    return jnp.concatenate([query, keys, values], axis=-1).reshape(lead + (-1,))
 
 
 def silu_slope(value):
@@ -112,21 +411,12 @@
     z_qkv = jnp.dot(flat, qkv_full, preferred_element_type=jnp.float32)
     mixed_f, hat_qkv, scale_qkv, total = norm_forward(z_qkv, weights, qkv_gains, qkv_shifts)
     mixed = mixed_f.astype(jnp.bfloat16).reshape(images, SLOT, HEADS, -1)
-    query = mixed[..., :KEY]
-    keys = mixed[..., KEY : 2 * KEY]
-    values = mixed[..., 2 * KEY :]
-    class_onehot = (classes[:, None] == jnp.arange(CLASSES)[None, :]).astype(jnp.float32)
-    class_bias = bias_table[:, offset_table]
-    bias = jnp.einsum("ic,hcqp->ihqp", class_onehot, class_bias, precision=lax.Precision.HIGHEST)
-    scores = attention_scores(query, keys, bias, keep)
-    top = jnp.max(scores, axis=-1, keepdims=True)
-    expo = jnp.exp(scores - top)
-    denom = jnp.sum(expo, axis=-1, keepdims=True)
-    probs = (expo / denom).astype(jnp.bfloat16)
-    log_total = top + jnp.log(denom)
-    attended = jnp.einsum(
-        "ihqp,iphv->iqhv", probs, values, preferred_element_type=jnp.float32
-    ).reshape(length, -1)
+    scaled = jnp.where(jnp.arange(KEY * 6) < KEY, KEY ** (-0.5) * LOG2E, 1.0)
+    mixed = arrange((mixed_f.reshape(images, SLOT, HEADS, -1) * scaled).astype(jnp.bfloat16).reshape(images, SLOT, -1))
+    mixed = jnp.pad(mixed, ((0, 0), (0, ROWS - SLOT), (0, 0)))
+    biases = bias_call(offset_table, bias_table)
+    attended_low, probs, shares = attend_call(classes, mixed, biases)
+    attended = attended_low[:, :SLOT].astype(jnp.float32).reshape(length, -1)
     activated = jax.nn.silu(attended).astype(jnp.bfloat16)
     z_out = jnp.dot(activated, out_full, preferred_element_type=jnp.float32)
     branch, hat_out, scale_out, unused_out = norm_forward(z_out, weights, out_gains, out_shifts)
@@ -161,27 +451,10 @@
     dz_out_low = dz_out.astype(jnp.bfloat16)
     out_grad = left_product(activated, dz_out_low)
     grad_att = (right_product(dz_out_low, out_full) * silu_slope(attended)).astype(jnp.bfloat16)
-    grad_att = grad_att.reshape(images, SLOT, HEADS, VALD)
-    again = attention_scores(query, keys, bias, keep)
-    prob_full = jnp.exp(again - log_total)
-    prob_low = prob_full.astype(jnp.bfloat16)
-    dprob = jnp.einsum("iqhv,iphv->ihqp", grad_att, values, preferred_element_type=jnp.float32)
-    grad_values = jnp.einsum(
-        "ihqp,iqhv->iphv", prob_low, grad_att, preferred_element_type=jnp.float32
-    )
-    dscore = prob_full * (dprob - jnp.sum(dprob * prob_full, axis=-1, keepdims=True))
-    per_class = jnp.einsum("ic,ihqp->cqph", class_onehot, dscore, precision=lax.Precision.HIGHEST)
-    local_table = jax.ops.segment_sum(
-        per_class.reshape(-1, HEADS), offset_table.reshape(-1), num_segments=NOFF
-    ).T
-    score_low = dscore.astype(jnp.bfloat16)
-    grad_query = jnp.einsum(
-        "ihqp,iphk->iqhk", score_low, keys, preferred_element_type=jnp.float32
-    ) * KEY ** (-0.5)
-    grad_keys = jnp.einsum(
-        "ihqp,iqhk->iphk", score_low, query, preferred_element_type=jnp.float32
-    ) * KEY ** (-0.5)
-    grad_mixed = jnp.concatenate([grad_query, grad_keys, grad_values], axis=-1).reshape(length, -1)
+    grad_att = jnp.pad(grad_att.reshape(images, SLOT, -1), ((0, 0), (0, ROWS - SLOT), (0, 0)))
+    grad_mixed, *accs = back_call(classes, mixed, probs, shares, grad_att, attended_low)
+    local_table = table_call(offset_table, accs)[:, :NOFF]
+    grad_mixed = restore(grad_mixed[:, :SLOT]).astype(jnp.float32).reshape(length, -1)
     dz_qkv, qkv_gain_grad, qkv_shift_grad = norm_backward(
         grad_mixed, hat_qkv, scale_qkv, total, qkv_gains, weights
     )

time: 3870 us -> 1060 us (0.27)
  other arithmetic: 2010 us -> 92.1 us
  local copies, waits for them, and re-layouts: 954 us -> 121 us
  matrix products: 125 us -> 47.1 us
  Pallas kernels: 0 us -> 44.9 us
    scatter-add x1 -> x0, other arithmetic: 1920 us -> none  [shards(): jax.ops.segment_sum(per_class.reshape(-1, HEADS), offset_table.reshape(-1...]
    gather x3 -> x0, local copies, waits for them, and re-layouts: 723 us -> none  [shards(): class_bias = bias_table[:, offset_table]]
    dot_general x8 -> x0, matrix products: 81.6 us -> none  [the longest x1 16.2 us: attention_scores(): jnp.einsum('iqhk,iphk->ihqp', query, keys, preferred_element_type=jnp.flo...]
    reshape x6 -> x8, local copies, waits for them, and re-layouts: 119 us -> 39.2 us  [the longest x1 11 us: shards(): mixed_f.reshape(images, SLOT, HEADS, -1) * scaled]
    pallas_call x0 -> x4, Pallas kernels: none -> 44.9 us  [the longest x1 18.4 us: back_call(): pl.pallas_call(back_kernel, grid_spec=pltpu.PrefetchScalarGridSpec(num_sc...]
  transfers between devices with their start and end apart: 5 -> 5, of which waited for: 5 -> 5; matrix products, arithmetic and copies ran while one was open for 1% -> 3% of each run, Pallas kernels for 0% -> 0%
where the time goes in v1:
time: 1060 us; the launch traced here: 1050 us
  blocking collectives  470 us (44%)
  waiting for transfers between devices  258 us (24%)
  local copies, waits for them, and re-layouts  121 us (11%)
  other arithmetic  92.1 us (9%)
  matrix products  47.1 us (4%)
  Pallas kernels  44.9 us (4%)
  between operations  16.5 us (2%)
    psum x4, blocking collectives, norm_backward(): lax.psum((jnp.sum(grad, axis=0), jnp.sum(grad * normed, axis=0)), ('dp',...  160 us
    psum x4, blocking collectives, norm_forward(): lax.psum((jnp.sum(value * weights, axis=0), jnp.sum(value * value * weigh...  157 us
    reduce_scatter x1, waiting for transfers between devices, shards(): lax.psum_scatter(whole[1].astype(jnp.bfloat16), 'fsdp', scatter_dimension...  64 us
    reduce_scatter x1, waiting for transfers between devices, shards(): lax.psum_scatter(whole[2].astype(jnp.bfloat16), 'fsdp', scatter_dimension...  63.6 us
    reduce_scatter x1, waiting for transfers between devices, shards(): lax.psum_scatter(whole[3].astype(jnp.bfloat16), 'fsdp', scatter_dimension...  62 us
    unnamed x6, waiting for transfers between devices  51.5 us
    all_gather x1, blocking collectives, shards(): lax.all_gather(down_weight, 'fsdp', axis=0, tiled=True)  33.3 us
    all_gather x1, blocking collectives, shards(): lax.all_gather(up_weight, 'fsdp', axis=0, tiled=True)  32.8 us
  transfers between devices with their start and end apart: 5, of which 5 were waited for; matrix products, arithmetic and copies ran while one was open for 3% of the time, Pallas kernels for 0%

profile of v1, /device:TPU:0, one launch (start us, length us, event | category | flops | bytes accessed | tf_op | source)
XLA Modules:
  0.0 1050.0 jit_solution(4778611458746558868)
XLA Ops:
  10.8 32.7 %all_gather.36 = bf16[256,768]{1,0:T(8,128)(2,1)S(1)} all-gather(bf16[32,768]{1,0:T(8,128)(2,1)S(1)} %copy-done.27), channel_id=1, replica_groups=mesh['dp'=4,'fsdp'=8] {'fsdp'}, dimensions={0}, use_global_device_ids=true | all-gather | bytes 442368 | tf_op jit(solution)/shard_map/all_gather | solution.py:387
  48.0 21.7 %all-reduce.18 = (bf16[768]{0:T(1024)(128)(2,1)S(1)}, bf16[768]{0:T(1024)(128)(2,1)S(1)}, bf16[256]{0:T(256)(128)(2,1)S(1)}, bf16[256]{0:T(256)(128)(2,1)S(1)}, ...) all-reduce(bf16[768]{0:T(1024)(128)(2,1)S(1)} %dynamic-update-slice, ...), channel_id=1, replica_groups=mesh['dp'=4,'fsdp'=8] {'fsdp'}, use_global_device_ids=true, to_apply=%add.3 | all-reduce | flops 3584 | bytes 14336
  73.9 37.3 %all-reduce.17 = (f32[768]{0:T(1024)S(1)}, f32[]{:T(128)}, f32[768]{0:T(1024)S(1)}) all-reduce(f32[768]{0:T(1024)S(1)} %get-tuple-element.81, f32[]{:T(128)} %fusion.8, f32[768]{0:T(1024)S(1)} %get-tuple-element.80), channel_id=1, replica_groups=mesh['dp'=4,'fsdp'=8] {'dp','fsdp'}, use_global_device_ids=true, to_apply=%region_5.6 | all-reduce | flops 1537 | bytes 12296 | tf_op jit(solution)/shard_map/psum | solution.py:323
  111.9 7.5 multiply_add_fusion
  119.4 8.8 copy.59
  128.3 11.0 %reshape.132 = f32[8,324,4,192]{1,0,3,2:T(8,128)} reshape(f32[2592,768]{0,1:T(8,128)} %copy.59) | data formatting | bytes 15925248 | tf_op jit(solution)/shard_map/reshape | solution.py:415
  155.6 9.3 shard_map.280
  168.6 12.0 %shard_map.281 = (bf16[8,336,512]{2,1,0:T(8,128)(2,1)}, bf16[8,336,1536]{2,1,0:T(8,128)(2,1)}, f32[8,336,128]{2,1,0:T(8,128)S(1)}) custom-call(s32[8]{0:T(128)S(1)} %copy-done.6, bf16[8,336,768]{2,1,0:T(8,128)(2,1)} %fusion.4.mixed_ref, f32[2,112,256]{2,1,0:T(8,128)S(1)} %get-tuple-element.25.bias0, f32[2,208,512]{2,1,0:T(8,128)S(1)} %get-tuple-element.26.bias1, ...), custom_call_target="tpu_custom_call" | custom-call | tf_op jit(solution)/shard_map/pallas_call | solution.py:254
  196.4 32.7 %all_gather.39 = bf16[512,256]{1,0:T(8,128)(2,1)} all-gather(bf16[64,256]{1,0:T(8,128)(2,1)S(1)} %copy-done.28), channel_id=1, replica_groups=mesh['dp'=4,'fsdp'=8] {'fsdp'}, dimensions={0}, use_global_device_ids=true | all-gather | bytes 294912 | tf_op jit(solution)/shard_map/all_gather | solution.py:390
  229.1 32.8 %all_gather.42 = bf16[256,512]{1,0:T(8,128)(2,1)} all-gather(bf16[32,512]{1,0:T(8,128)(2,1)S(1)} %copy-done.29), channel_id=1, replica_groups=mesh['dp'=4,'fsdp'=8] {'fsdp'}, dimensions={0}, use_global_device_ids=true | all-gather | bytes 294912 | tf_op jit(solution)/shard_map/all_gather | solution.py:393
  261.9 33.3 %all_gather.45 = bf16[512,256]{1,0:T(8,128)(2,1)} all-gather(bf16[64,256]{1,0:T(8,128)(2,1)S(1)} %copy-done.30), channel_id=1, replica_groups=mesh['dp'=4,'fsdp'=8] {'fsdp'}, dimensions={0}, use_global_device_ids=true | all-gather | bytes 294912 | tf_op jit(solution)/shard_map/all_gather | solution.py:396
  306.1 39.3 %all-reduce.16 = (f32[256]{0:T(256)S(1)}, f32[256]{0:T(256)S(1)}) all-reduce(f32[256]{0:T(256)S(1)} %get-tuple-element.89, f32[256]{0:T(256)S(1)} %get-tuple-element.88), channel_id=1, replica_groups=mesh['dp'=4,'fsdp'=8] {'dp','fsdp'}, use_global_device_ids=true, to_apply=%region_7.8 | all-reduce | flops 512 | bytes 4096 | tf_op jit(solution)/shard_map/psum | solution.py:323
  352.8 40.9 %all-reduce.15 = (f32[512]{0:T(512)S(1)}, f32[512]{0:T(512)S(1)}) all-reduce(f32[512]{0:T(512)S(1)} %get-tuple-element.83, f32[512]{0:T(512)S(1)} %get-tuple-element.82), channel_id=1, replica_groups=mesh['dp'=4,'fsdp'=8] {'dp','fsdp'}, use_global_device_ids=true, to_apply=%region_13.14 | all-reduce | flops 1024 | bytes 8192 | tf_op jit(solution)/shard_map/psum | solution.py:323
  401.1 39.0 %all-reduce.14 = (f32[256]{0:T(256)S(1)}, f32[256]{0:T(256)S(1)}) all-reduce(f32[256]{0:T(256)S(1)} %get-tuple-element.87, f32[256]{0:T(256)S(1)} %get-tuple-element.86), channel_id=1, replica_groups=mesh['dp'=4,'fsdp'=8] {'dp','fsdp'}, use_global_device_ids=true, to_apply=%region_15.16 | all-reduce | flops 512 | bytes 4096 | tf_op jit(solution)/shard_map/psum | solution.py:323
  443.8 41.0 %all-reduce.13 = (f32[256]{0:T(256)S(1)}, f32[256]{0:T(256)S(1)}) all-reduce(f32[256]{0:T(256)S(1)} %multiply_reduce_fusion.7, f32[256]{0:T(256)S(1)} %multiply_reduce_fusion.8), channel_id=1, replica_groups=mesh['dp'=4,'fsdp'=8] {'dp','fsdp'}, use_global_device_ids=true, to_apply=%region_21.22 | all-reduce | flops 512 | bytes 4096 | tf_op jit(solution)/shard_map/psum | solution.py:340
  488.6 6.9 fusion.10
  495.5 39.2 %all-reduce.12 = (f32[512]{0:T(512)S(1)}, f32[512]{0:T(512)S(1)}) all-reduce(f32[512]{0:T(512)S(1)} %get-tuple-element.85, f32[512]{0:T(512)S(1)} %get-tuple-element.84), channel_id=1, replica_groups=mesh['dp'=4,'fsdp'=8] {'dp','fsdp'}, use_global_device_ids=true, to_apply=%region_25.26 | all-reduce | flops 1024 | bytes 8192 | tf_op jit(solution)/shard_map/psum | solution.py:340
  534.7 6.4 multiply_convert_fusion.3
  543.7 40.8 %all-reduce.11 = (f32[256]{0:T(256)S(1)}, f32[256]{0:T(256)S(1)}) all-reduce(f32[256]{0:T(256)S(1)} %get-tuple-element.91, f32[256]{0:T(256)S(1)} %get-tuple-element.90), channel_id=1, replica_groups=mesh['dp'=4,'fsdp'=8] {'dp','fsdp'}, use_global_device_ids=true, to_apply=%region_29.30 | all-reduce | flops 512 | bytes 4096 | tf_op jit(solution)/shard_map/psum | solution.py:340
  604.9 18.4 %shard_map.282 = (bf16[8,336,768]{2,1,0:T(8,128)(2,1)}, f32[2,112,256]{2,1,0:T(8,128)S(1)}, f32[2,208,512]{2,1,0:T(8,128)S(1)}, f32[2,336,768]{2,1,0:T(8,128)S(1)}) custom-call(s32[8]{0:T(128)S(1)} %copy-done.6, bf16[8,336,768]{2,1,0:T(8,128)(2,1)} %fusion.4.mixed_ref, bf16[8,336,1536]{2,1,0:T(8,128)(2,1)} %get-tuple-element.29.p_ref, ...), custom_call_target="tpu_custom_call" | custom-call | tf_op jit(solution)/shard_map/pallas_call | solution.py:274
  644.1 7.0 fusion.9
  651.1 8.1 maximum_convert_fusion
  659.3 12.6 %copy.87 = f32[8,324,4,192]{3,2,1,0:T(4,128)} copy(f32[8,324,4,192]{3,0,2,1:T(8,128)} %maximum_convert_fusion) | data formatting | bytes 15925248 | tf_op jit(solution)/shard_map/convert_element_type | solution.py:457
  671.9 12.6 %reshape.191 = f32[2592,768]{1,0:T(8,128)} reshape(f32[8,324,4,192]{3,2,1,0:T(4,128)} %copy.87) | data formatting | bytes 15925248 | tf_op jit(solution)/shard_map/convert_element_type | solution.py:457
  684.5 6.8 multiply_reduce_fusion
  696.5 39.2 %all-reduce.10 = (f32[768]{0:T(1024)S(1)}, f32[768]{0:T(1024)S(1)}, f32[4,324]{1,0:T(4,128)}) all-reduce(f32[768]{0:T(1024)S(1)} %multiply_reduce_fusion, f32[768]{0:T(1024)S(1)} %reduce_sum.183, f32[4,324]{1,0:T(4,128)S(1)} %bitcast.41), channel_id=1, replica_groups=mesh['dp'=4,'fsdp'=8] {'dp','fsdp'}, use_global_device_ids=true, to_apply=%region_33.34 | all-reduce | flops 2832 | bytes 22656 | tf_op jit(solution)/shard_map/psum | solution.py:340
  735.7 7.9 multiply_convert_fusion.1
  760.9 51.4 %reduce-scatter.13.cloned.1.call-done = bf16[32,768]{1,0:T(8,128)(2,1)} async-done(((bf16[256,768]{1,0:T(8,128)(2,1)}), bf16[32,768]{1,0:T(8,128)(2,1)}) %reduce-scatter.13.cloned.1.call-update) | async-done | bytes 49168
  814.0 62.0 %reduce-scatter.11.cloned.1.call-done = bf16[64,256]{1,0:T(8,128)(2,1)} async-done(((bf16[512,256]{1,0:T(8,128)(2,1)}), bf16[64,256]{1,0:T(8,128)(2,1)}) %reduce-scatter.11.cloned.1.call-update) | async-done | bytes 32784 | tf_op jit(solution)/shard_map/reduce_scatter | solution.py:481
  875.9 63.6 %reduce-scatter.9.cloned.1.call-done = bf16[32,512]{1,0:T(8,128)(2,1)} async-done(((bf16[256,512]{1,0:T(8,128)(2,1)}), bf16[32,512]{1,0:T(8,128)(2,1)}) %reduce-scatter.9.cloned.1.call-update) | async-done | bytes 32784 | tf_op jit(solution)/shard_map/reduce_scatter | solution.py:478
  939.5 64.0 %reduce-scatter.7.cloned.1.call-done = bf16[64,256]{1,0:T(8,128)(2,1)} async-done(((bf16[512,256]{1,0:T(8,128)(2,1)}), bf16[64,256]{1,0:T(8,128)(2,1)}) %reduce-scatter.7.cloned.1.call-update) | async-done | bytes 32784 | tf_op jit(solution)/shard_map/reduce_scatter | solution.py:475
  1020.1 17.3 %all-reduce.22.cloned.1.call-done = (bf16[32,768]{0,1:T(8,128)(2,1)}, bf16[64,256]{1,0:T(8,128)(2,1)}, bf16[32,512]{1,0:T(8,128)(2,1)}, bf16[64,256]{1,0:T(8,128)(2,1)}) async-done(((bf16[32,768]{0,1:T(8,128)(2,1)}, bf16[64,256]{1,0:T(8,128)(2,1)}, bf16[32,512]{1,0:T(8,128)(2,1)}, bf16[64,256]{1,0:T(8,128)(2,1)}), (bf16[32,768]{0,1:T(8,128)(2,1)}, bf16[64,256]{1,0:T(8,128)(2,1)}, bf16[32,512]{1,0:T(8,128)(2,1)}, ...) | async-done | bytes 147472 | tf_op jit(solution)/shard_map/psum | solution.py:466
  (193 shorter events, 169.9 us)
Async XLA Ops:
  7.2 805.2 %reduce-scatter.13.cloned.1.call-start = ((), (), s32[]{:S(2)}) async-start(), calls=%async_computation.7 | async-start | bytes 442368
  8.7 34.8 %copy-start.43 = (u32[32]{0:T(128)S(1)}, u32[32]{0:T(128)}, u32[]{:S(2)}) copy-start(u32[32]{0:T(128)} %constant.53) | copy-start | bytes 388
  8.7 37.3 %copy-start.35 = (bf16[32]{0:T(256)(128)(2,1)S(1)}, bf16[32]{0:T(256)(128)(2,1)}, u32[]{:S(2)}) copy-start(bf16[32]{0:T(256)(128)(2,1)} %param.25) | copy-start | bytes 196
  8.7 37.6 %copy-start.36 = (bf16[32]{0:T(256)(128)(2,1)S(1)}, bf16[32]{0:T(256)(128)(2,1)}, u32[]{:S(2)}) copy-start(bf16[32]{0:T(256)(128)(2,1)} %param.26) | copy-start | bytes 196
  8.8 37.8 %copy-start.37 = (bf16[32]{0:T(256)(128)(2,1)S(1)}, bf16[32]{0:T(256)(128)(2,1)}, u32[]{:S(2)}) copy-start(bf16[32]{0:T(256)(128)(2,1)} %param.31) | copy-start | bytes 196
  8.8 38.0 %copy-start.38 = (bf16[32]{0:T(256)(128)(2,1)S(1)}, bf16[32]{0:T(256)(128)(2,1)}, u32[]{:S(2)}) copy-start(bf16[32]{0:T(256)(128)(2,1)} %param.32) | copy-start | bytes 196
  8.8 38.3 %copy-start.39 = (bf16[96]{0:T(256)(128)(2,1)S(1)}, bf16[96]{0:T(256)(128)(2,1)}, u32[]{:S(2)}) copy-start(bf16[96]{0:T(256)(128)(2,1)} %param.22) | copy-start | bytes 580
  8.8 38.5 %copy-start.40 = (bf16[96]{0:T(256)(128)(2,1)S(1)}, bf16[96]{0:T(256)(128)(2,1)}, u32[]{:S(2)}) copy-start(bf16[96]{0:T(256)(128)(2,1)} %param.23) | copy-start | bytes 580
  8.8 38.7 %copy-start.41 = (bf16[64]{0:T(256)(128)(2,1)S(1)}, bf16[64]{0:T(256)(128)(2,1)}, u32[]{:S(2)}) copy-start(bf16[64]{0:T(256)(128)(2,1)} %param.28) | copy-start | bytes 388
  8.8 39.0 %copy-start.42 = (bf16[64]{0:T(256)(128)(2,1)S(1)}, bf16[64]{0:T(256)(128)(2,1)}, u32[]{:S(2)}) copy-start(bf16[64]{0:T(256)(128)(2,1)} %param.29) | copy-start | bytes 388
  10.8 63.2 %copy-start.14 = (bf16[2592,256]{1,0:T(8,128)(2,1)}, bf16[2592,256]{1,0:T(8,128)(2,1)S(1)}, u32[]{:S(2)}) copy-start(bf16[2592,256]{1,0:T(8,128)(2,1)S(1)} %reshape.131) | copy-start | bytes 3981316
  190.9 38.2 %copy-start.29 = (bf16[32,512]{1,0:T(8,128)(2,1)S(1)}, bf16[32,512]{1,0:T(8,128)(2,1)}, u32[]{:S(2)}) copy-start(bf16[32,512]{1,0:T(8,128)(2,1)} %param.27) | copy-start | bytes 98308
  190.9 71.0 %copy-start.30 = (bf16[64,256]{1,0:T(8,128)(2,1)S(1)}, bf16[64,256]{1,0:T(8,128)(2,1)}, u32[]{:S(2)}) copy-start(bf16[64,256]{1,0:T(8,128)(2,1)} %param.30) | copy-start | bytes 98308
  190.9 104.3 %copy-start.20 = (bf16[8,324,256]{2,0,1:T(8,128)(2,1)S(1)}, bf16[8,324,256]{2,0,1:T(8,128)(2,1)}, u32[]{:S(2)}) copy-start(bf16[8,324,256]{2,0,1:T(8,128)(2,1)} %param.33) | copy-start | bytes 3981316
  488.6 6.9 copy-start.21
  534.7 6.4 copy-start.8
  534.7 6.4 copy-start.13
  534.7 6.4 copy-start.23
  584.5 6.3 copy-start.33
  584.5 7.4 copy-start.24
  644.1 7.0 copy-start.10
  644.1 7.0 copy-start.11
  644.1 7.0 copy-start.12
  684.5 6.8 copy-start.2
  684.5 6.8 copy-start.4
  735.7 9.8 copy-start.15
  749.7 126.2 %reduce-scatter.11.cloned.1.call-start = ((), (), s32[]{:S(2)}) async-start(), calls=%async_computation.6 | async-start | bytes 294912 | tf_op jit(solution)/shard_map/reduce_scatter | solution.py:481
  753.6 186.0 %reduce-scatter.9.cloned.1.call-start = ((), (), s32[]{:S(2)}) async-start(), calls=%async_computation.5 | async-start | bytes 294912 | tf_op jit(solution)/shard_map/reduce_scatter | solution.py:478
  756.6 247.0 %copy-start.9 = (f32[2592,256]{1,0:T(8,128)S(1)}, f32[2592,256]{1,0:T(8,128)}, u32[]{:S(2)}) copy-start(f32[2592,256]{1,0:T(8,128)} %get-tuple-element.141) | copy-start | bytes 7962628
  756.6 246.9 %reduce-scatter.7.cloned.1.call-start = ((), (), s32[]{:S(2)}) async-start(), calls=%async_computation.4 | async-start | bytes 294912 | tf_op jit(solution)/shard_map/reduce_scatter | solution.py:475
  760.9 276.6 %all-reduce.22.cloned.1.call-start = ((), (), s32[]{:S(2)}) async-start(), calls=%async_computation.8 | async-start | bytes 589824 | tf_op jit(solution)/shard_map/psum | solution.py:466
  1003.6 6.6 copy-start.32
  (17 other events, 64.2 us)
Sparse Core Ops, SparseCore 0:
  749.8 62.4 reduce-scatter.12
  815.7 60.2 reduce-scatter.10
  879.3 60.2 reduce-scatter.8
  943.3 60.2 reduce-scatter.6
  1005.9 31.4 all-reduce.21

commit v2 on v1

--- a/solution.py
+++ b/solution.py
@@ -1,3 +1,5 @@
+import functools
+
 import jax
 import jax.numpy as jnp
 from jax import lax
@@ -226,21 +228,6 @@
     return jnp.concatenate(rows_out, axis=0)
 
 
-def bias_kernel(off_ref, table_ref, out0, out1, out2, index_ref):
-    bias_tables(off_ref, table_ref, index_ref, (out0, out1, out2))
-
-
-def bias_call(offset_table, bias_table):
-    return pl.pallas_call(
-        bias_kernel,
-        out_shape=[jax.ShapeDtypeStruct((2, r, 2 * l), jnp.float32) for _, _, r, l in PARTS],
-        in_specs=[VMEM, VMEM],
-        out_specs=[VMEM] * 3,
-        scratch_shapes=[pltpu.VMEM((ROWS, 384), jnp.int32)],
-        compiler_params=pltpu.CompilerParams(vmem_limit_bytes=48 * 2**20),
-    )(offset_table, bias_table)
-
-
 def image_spec(width):
     return pl.BlockSpec((1, ROWS, width), lambda i, c: (i, 0, 0))
 
@@ -299,19 +286,312 @@
     )(offset_table, *accs)
 
 
+MESH = pl.DeviceIdType.MESH
+ANY = pl.BlockSpec(memory_space=pl.ANY)
+SMEM = pl.BlockSpec(memory_space=pltpu.SMEM)
+
+
+class Place:
+    def __init__(self, dp_size, fs_size):
+        self.dp_size, self.fs_size = dp_size, fs_size
+        self.size = dp_size * fs_size
+        self.dp, self.fs = lax.axis_index("dp"), lax.axis_index("fsdp")
+        self.me = self.dp * fs_size + self.fs
+        self.core = lax.rem(self.dp, 2)
+        self.partner = (self.dp + 1 - 2 * self.core, self.fs)
+
+    def other(self, step):
+        spot = lax.rem(self.me + step, self.size)
+        return (spot // self.fs_size, lax.rem(spot, self.fs_size))
+
+    def greet(self):
+        barrier = pltpu.get_barrier_semaphore()
+
+        def signal(step, _):
+            pl.semaphore_signal(barrier, inc=1, device_id=self.other(step), device_id_type=MESH)
+            return 0
+
+        lax.fori_loop(1, self.size, signal, 0)
+
+    def meet(self):
+        pl.semaphore_wait(pltpu.get_barrier_semaphore(), self.size - 1)
+
+    def spread(self, buf, value, send, recv):
+        buf[self.me] = value
+
+        def start(step, _):
+            push(buf.at[self.me], buf.at[self.me], send, recv, self.other(step))
+            return 0
+
+        lax.fori_loop(1, self.size, start, 0)
+
+    def collect(self, buf, recv):
+        await_bytes(buf.at[pl.ds(0, self.size - 1)], recv)
+        return jnp.sum(buf[...], axis=0)
+
+    def settle(self, buf, send):
+        await_bytes(buf.at[pl.ds(0, self.size - 1)], send)
+
+
+def push(source, target, send, recv, device):
+    pltpu.make_async_remote_copy(
+        src_ref=source, dst_ref=target, send_sem=send, recv_sem=recv, device_id=device, device_id_type=MESH
+    ).start()
+
+
+def await_bytes(ref, sem):
+    pltpu.make_async_copy(ref, ref, sem).wait()
+
+
+def halves(width):
+    return (width // 2,) * 2
+
+
+def gather_start(place, buf, send, recv):
+    half = buf.shape[2] // 2
+
+    def start(step, _):
+        target = lax.rem(place.fs + step, place.fs_size)
+        for core in range(2):
+
+            @pl.when(place.core == core)
+            def _():
+                part = buf.at[place.fs, :, pl.ds(core * half, half)]
+                push(part, part, send, recv, (place.dp, target))
+
+        return 0
+
+    lax.fori_loop(1, place.fs_size, start, 0)
+
+
+def gather_pass(place, buf, recv, send2, recv2):
+    half = buf.shape[2] // 2
+    for core in range(2):
+
+        @pl.when(place.core == core)
+        def _():
+            await_bytes(buf.at[pl.ds(0, place.fs_size - 1), :, pl.ds(core * half, half)], recv)
+            part = buf.at[:, :, pl.ds(core * half, half)]
+            push(part, part, send2, recv2, place.partner)
+
+
+def gather_end(place, buf, recv2):
+    half = buf.shape[2] // 2
+    await_bytes(buf.at[:, :, pl.ds(0, half)], recv2)
+
+
+def gather_settle(place, buf, send, send2):
+    half = buf.shape[2] // 2
+    await_bytes(buf.at[pl.ds(0, place.fs_size - 1), :, pl.ds(0, half)], send)
+    await_bytes(buf.at[:, :, pl.ds(0, half)], send2)
+
+
+def flat_weight(buf):
+    shards, rows, width = buf.shape
+    if rows % 16 == 0:
+        return buf[...].reshape(shards * rows, width)
+    wide = jnp.concatenate([buf[k].astype(jnp.float32) for k in range(shards)], axis=0)
+    return wide.astype(jnp.bfloat16)
+
+
+def split_low(value):
+    high = value.astype(jnp.bfloat16)
+    return high, (value - high.astype(jnp.float32)).astype(jnp.bfloat16)
+
+
+def precise(left, right):
+    high, low = split_low(left)
+    return dot_nn(high, right) + dot_nn(low, right)
+
+
 def arrange(columns):
-    lead = columns.shape[:-1]
-    heads = columns.reshape(lead + (HEADS, 2 * KEY + VALD))
-    parts = (heads[..., :KEY], heads[..., KEY : 2 * KEY], heads[..., 2 * KEY :])
-    return jnp.concatenate([part.reshape(lead + (-1,)) for part in parts], axis=-1)
+    blocks = [columns[:, (2 * KEY + VALD) * h : (2 * KEY + VALD) * (h + 1)] for h in range(HEADS)]
+    parts = [b[:, :KEY] for b in blocks] + [b[:, KEY : 2 * KEY] for b in blocks] + [b[:, 2 * KEY :] for b in blocks]
+    return jnp.concatenate(parts, axis=1)
 
 
 def restore(columns):
-    lead = columns.shape[:-1]
-    query = columns[..., :128].reshape(lead + (HEADS, KEY))
-    keys = columns[..., 128:256].reshape(lead + (HEADS, KEY))
-    values = columns[..., 256:].reshape(lead + (HEADS, VALD))
-    return jnp.concatenate([query, keys, values], axis=-1).reshape(lead + (-1,))
+    parts = []
+    for h in range(HEADS):
+        parts += [
+            columns[:, KEY * h : KEY * (h + 1)],
+            columns[:, 128 + KEY * h : 128 + KEY * (h + 1)],
+            columns[:, 256 + VALD * h : 256 + VALD * (h + 1)],
+        ]
+    return jnp.concatenate(parts, axis=1)
+
+
+def limits_of(kind):
+    return jnp.where(kind == 0, (GRID - 8) ** 2, jnp.where(kind == 1, (GRID - 4) ** 2, SLOT))
+
+
+def assemble(buf, widths, lanes):
+    turned = {}
+    for width in sorted(set(widths)):
+        turned[width] = sum(
+            pltpu.roll(pad_lanes(buf[k], lanes), k * width, 1) if k else pad_lanes(buf[k], lanes)
+            for k in range(buf.shape[0])
+        )
+    return [turned[width][k : k + 1] for k, width in enumerate(widths)]
+
+
+def first_kernel(dp_size, fs_size, *refs):
+    class_ref, x_ref, off_ref, table_ref = refs[:4]
+    shards, vectors = refs[4:8], refs[8:16]
+    mixed_out, xs_out, bias_out, weight_out, vec_out = refs[16], refs[17], refs[18:21], refs[21:25], refs[25]
+    xs, z, mixed, index = refs[26:30]
+    bias, weights = refs[30:33], refs[33:37]
+    vbuf, stat = refs[37:39]
+    send, recv, send2, recv2, local = refs[39:44]
+    place = Place(dp_size, fs_size)
+    images = x_ref.shape[0]
+
+    for k in range(4):
+        own = shards[k][...]
+        if k == 0:
+            own = arrange(own.astype(jnp.float32)).astype(jnp.bfloat16)
+        weights[k][place.fs] = own
+    vbuf[place.fs] = jnp.concatenate(
+        [pad_lanes(v[...].astype(jnp.float32), 128) for v in vectors], axis=0
+    )
+    place.greet()
+
+    def load(image, count):
+        limit = limits_of(class_ref[image])
+        row = lax.broadcasted_iota(jnp.int32, (SLOT, 1), 0)
+        value = jnp.where(row < limit, x_ref[image].astype(jnp.float32), 0.0)
+        xs[image] = pad_rows(value, ROWS).astype(jnp.bfloat16)
+        return count + limit
+
+    count = lax.fori_loop(0, images, load, 0)
+    flat = xs[...].reshape(images * ROWS, xs.shape[2])
+    gram = dot_tn(flat, flat)
+    total_x = dot_nn(jnp.ones((8, images * ROWS), jnp.bfloat16), flat)
+
+    place.meet()
+    gather_start(place, weights[0], send.at[0], recv.at[0])
+
+    def start(step, _):
+        target = lax.rem(place.fs + step, place.fs_size)
+        push(vbuf.at[place.fs], vbuf.at[place.fs], send.at[4], recv.at[4], (place.dp, target))
+        return 0
+
+    lax.fori_loop(1, place.fs_size, start, 0)
+    for k in range(1, 4):
+        gather_start(place, weights[k], send.at[k], recv.at[k])
+    xs_copy = pltpu.make_async_copy(xs, xs_out, local.at[0])
+    xs_copy.start()
+    bias_tables(off_ref, table_ref, index, bias)
+    copies = [xs_copy]
+    for k in range(3):
+        copies.append(pltpu.make_async_copy(bias[k], bias_out[k], local.at[1 + k]))
+        copies[-1].start()
+
+    gather_pass(place, weights[0], recv.at[0], send2.at[0], recv2.at[0])
+    gather_end(place, weights[0], recv2.at[0])
+    weight = flat_weight(weights[0])
+    high, low = split_low(gram)
+    spread = dot_nn(high, weight) + dot_nn(low, weight)
+    squares = jnp.sum(weight.astype(jnp.float32) * spread, axis=0, keepdims=True)
+    sums = precise(total_x, weight)[:1]
+    tail = jnp.full((1, 128), count.astype(jnp.float32))
+    place.spread(
+        stat,
+        jnp.concatenate(
+            [jnp.concatenate([sums, tail], axis=1), jnp.concatenate([squares, tail], axis=1)], axis=0
+        ),
+        send.at[5],
+        recv.at[5],
+    )
+
+    def product(image, _):
+        z[image] = dot_nn(xs[image], weight)
+        return 0
+
+    lax.fori_loop(0, images, product, 0)
+    for k in range(1, 4):
+        gather_pass(place, weights[k], recv.at[k], send2.at[k], recv2.at[k])
+    await_bytes(vbuf.at[pl.ds(0, place.fs_size - 1)], recv.at[4])
+    widths = [v.shape[1] for v in vectors]
+    full = assemble(vbuf, widths, 768)
+    full[0], full[1] = arrange(full[0]), arrange(full[1])
+
+    got = place.collect(stat, recv.at[5])
+    whole = got[0:1, 768:769]
+    center = got[0:1, :768] / whole
+    square = got[1:2, :768] / whole
+    scale = lax.rsqrt(square - center * center + EPS)
+    vec_out[...] = jnp.concatenate(
+        full + [scale, center, jnp.broadcast_to(whole, (1, 768)), jnp.zeros((5, 768), jnp.float32)], axis=0
+    )
+    gain = scale * full[0]
+    shift = full[1] - center * gain
+    fold = jnp.where(lax.broadcasted_iota(jnp.int32, (1, 768), 1) < 128, KEY ** (-0.5) * LOG2E, 1.0)
+    gain, shift = gain * fold, shift * fold
+
+    def normal(image, _):
+        mixed[image] = (z[image] * gain + shift).astype(jnp.bfloat16)
+        pltpu.make_async_copy(mixed.at[image], mixed_out.at[image], local.at[8 + image]).start()
+        return 0
+
+    lax.fori_loop(0, images, normal, 0)
+    for k in range(4):
+        if k > 0:
+            gather_end(place, weights[k], recv2.at[k])
+        copies.append(pltpu.make_async_copy(weights[k], weight_out[k], local.at[4 + k]))
+        copies[-1].start()
+    for k in range(4):
+        gather_settle(place, weights[k], send.at[k], send2.at[k])
+    await_bytes(vbuf.at[pl.ds(0, place.fs_size - 1)], send.at[4])
+    place.settle(stat, send.at[5])
+    for copy in copies:
+        copy.wait()
+
+    def finish(image, _):
+        pltpu.make_async_copy(mixed.at[image], mixed_out.at[image], local.at[8 + image]).wait()
+        return 0
+
+    lax.fori_loop(0, images, finish, 0)
+
+
+def first_call(dp_size, fs_size, classes, inputs, offset_table, bias_table, weights, vectors):
+    images, model = inputs.shape[0], inputs.shape[2]
+    vectors = [v.reshape(1, -1) for v in vectors]
+    shapes = [(fs_size,) + w.shape for w in weights]
+    biases = [(2, r, 2 * l) for _, _, r, l in PARTS]
+    bf, f32 = jnp.bfloat16, jnp.float32
+    return pl.pallas_call(
+        functools.partial(first_kernel, dp_size, fs_size),
+        out_shape=[
+            jax.ShapeDtypeStruct((images, ROWS, 768), bf),
+            jax.ShapeDtypeStruct((images, ROWS, model), bf),
+        ]
+        + [jax.ShapeDtypeStruct(s, f32) for s in biases]
+        + [jax.ShapeDtypeStruct(s, bf) for s in shapes]
+        + [jax.ShapeDtypeStruct((16, 768), f32)],
+        in_specs=[SMEM] + [VMEM] * 15,
+        out_specs=[ANY] * 9 + [VMEM],
+        scratch_shapes=[
+            pltpu.VMEM((images, ROWS, model), bf),
+            pltpu.VMEM((images, ROWS, 768), f32),
+            pltpu.VMEM((images, ROWS, 768), bf),
+            pltpu.VMEM((ROWS, 384), jnp.int32),
+        ]
+        + [pltpu.VMEM(s, f32) for s in biases]
+        + [pltpu.VMEM(s, bf) for s in shapes]
+        + [
+            pltpu.VMEM((fs_size, 8, 128), f32),
+            pltpu.VMEM((dp_size * fs_size, 2, 896), f32),
+            pltpu.SemaphoreType.DMA((6,)),
+            pltpu.SemaphoreType.DMA((6,)),
+            pltpu.SemaphoreType.DMA((4,)),
+            pltpu.SemaphoreType.DMA((4,)),
+            pltpu.SemaphoreType.DMA((8 + images,)),
+        ],
+        compiler_params=pltpu.CompilerParams(
+            collective_id=0, has_side_effects=True, vmem_limit_bytes=56 * 2**20
+        ),
+    )(classes, inputs, offset_table, bias_table, *weights, *vectors)
 
 
 def silu_slope(value):
@@ -383,21 +663,17 @@
     down_shift,
     cotangent,
 ):
-    gathered = (
-        lax.all_gather(qkv_weight, "fsdp", axis=0, tiled=True),
-        lax.all_gather(qkv_gain, "fsdp", axis=0, tiled=True),
-        lax.all_gather(qkv_shift, "fsdp", axis=0, tiled=True),
-        lax.all_gather(out_weight, "fsdp", axis=0, tiled=True),
-        lax.all_gather(out_gain, "fsdp", axis=0, tiled=True),
-        lax.all_gather(out_shift, "fsdp", axis=0, tiled=True),
-        lax.all_gather(up_weight, "fsdp", axis=0, tiled=True),
-        lax.all_gather(up_gain, "fsdp", axis=0, tiled=True),
-        lax.all_gather(up_shift, "fsdp", axis=0, tiled=True),
-        lax.all_gather(down_weight, "fsdp", axis=0, tiled=True),
-        lax.all_gather(down_gain, "fsdp", axis=0, tiled=True),
-        lax.all_gather(down_shift, "fsdp", axis=0, tiled=True),
-    )
-    qkv_full, qkv_gains, qkv_shifts, out_full, out_gains, out_shifts = gathered[:6]
+    dp_size, fs_size = lax.axis_size("dp"), lax.axis_size("fsdp")
+    first = first_call(dp_size, fs_size, classes, inputs, offset_table, bias_table,
+        (qkv_weight, out_weight, up_weight, down_weight),
+        (qkv_gain, qkv_shift, out_gain, out_shift, up_gain, up_shift, down_gain, down_shift))
+    mixed, xs, biases, weights_full, vec = first[0], first[1], first[2:5], first[5:9], first[9]
+    qkv_full, out_full, up_full, down_full = [w.reshape(-1, w.shape[2]) for w in weights_full]
+    qkv_gains, qkv_shifts = vec[0], vec[1]
+    out_gains, out_shifts = vec[2, :256], vec[3, :256]
+    up_gains, up_shifts = vec[4, :512], vec[5, :512]
+    down_gains, down_shifts = vec[6, :256], vec[7, :256]
+    total = vec[10, 0]
     images = inputs.shape[0]
     length = images * SLOT
     limits = jnp.where(
@@ -409,12 +685,7 @@
     weights = keep.reshape(-1, 1)
     flat = inputs.reshape(length, -1)
     z_qkv = jnp.dot(flat, qkv_full, preferred_element_type=jnp.float32)
-    mixed_f, hat_qkv, scale_qkv, total = norm_forward(z_qkv, weights, qkv_gains, qkv_shifts)
-    mixed = mixed_f.astype(jnp.bfloat16).reshape(images, SLOT, HEADS, -1)
-    scaled = jnp.where(jnp.arange(KEY * 6) < KEY, KEY ** (-0.5) * LOG2E, 1.0)
-    mixed = arrange((mixed_f.reshape(images, SLOT, HEADS, -1) * scaled).astype(jnp.bfloat16).reshape(images, SLOT, -1))
-    mixed = jnp.pad(mixed, ((0, 0), (0, ROWS - SLOT), (0, 0)))
-    biases = bias_call(offset_table, bias_table)
+    hat_qkv, scale_qkv = (z_qkv - vec[9]) * vec[8], vec[8]
     attended_low, probs, shares = attend_call(classes, mixed, biases)
     attended = attended_low[:, :SLOT].astype(jnp.float32).reshape(length, -1)
     activated = jax.nn.silu(attended).astype(jnp.bfloat16)
@@ -422,8 +693,6 @@
     branch, hat_out, scale_out, unused_out = norm_forward(z_out, weights, out_gains, out_shifts)
     middle = flat.astype(jnp.float32) + branch
     middle_low = middle.astype(jnp.bfloat16)
-    second = gathered[6:]
-    up_full, up_gains, up_shifts, down_full, down_gains, down_shifts = second
     z_up = jnp.dot(middle_low, up_full, preferred_element_type=jnp.float32)
     up_normed, hat_up, scale_up, unused_up = norm_forward(z_up, weights, up_gains, up_shifts)
     hidden = jax.nn.silu(up_normed).astype(jnp.bfloat16)
@@ -454,12 +723,15 @@
     grad_att = jnp.pad(grad_att.reshape(images, SLOT, -1), ((0, 0), (0, ROWS - SLOT), (0, 0)))
     grad_mixed, *accs = back_call(classes, mixed, probs, shares, grad_att, attended_low)
     local_table = table_call(offset_table, accs)[:, :NOFF]
-    grad_mixed = restore(grad_mixed[:, :SLOT]).astype(jnp.float32).reshape(length, -1)
+    grad_mixed = grad_mixed[:, :SLOT].astype(jnp.float32).reshape(length, -1)
     dz_qkv, qkv_gain_grad, qkv_shift_grad = norm_backward(
         grad_mixed, hat_qkv, scale_qkv, total, qkv_gains, weights
     )
     dz_qkv_low = dz_qkv.astype(jnp.bfloat16)
     qkv_grad = left_product(flat, dz_qkv_low)
+    qkv_grad = restore(qkv_grad)
+    qkv_gain_grad = restore(qkv_gain_grad[None])[0]
+    qkv_shift_grad = restore(qkv_shift_grad[None])[0]
     input_grad = (grad_middle + right_product(dz_qkv_low, qkv_full)).reshape(inputs.shape)
     table_grad = lax.psum(local_table, ("dp", "fsdp"))
     whole = (

time: 1060 us -> 797 us (0.75)
  blocking collectives: 470 us -> 281 us
  local copies, waits for them, and re-layouts: 121 us -> 65.4 us
  other arithmetic: 92.1 us -> 59.4 us
  Pallas kernels: 44.9 us -> 66.8 us
    all_gather x4 -> x0, blocking collectives: 132 us -> none  [the longest x1 33.3 us: shards(): lax.all_gather(down_weight, 'fsdp', axis=0, tiled=True)]
    psum x4 -> x3, blocking collectives: 157 us -> 120 us  [norm_forward(): lax.psum((jnp.sum(value * weights, axis=0), jnp.sum(value * value * weigh...]
    pallas_call x1, Pallas kernels: 9.29 us -> 32.5 us  [first_call(): pl.pallas_call(functools.partial(first_kernel, dp_size, fs_size), out_sha...]
    unnamed x6, waiting for transfers between devices: 51.5 us -> 29.1 us
    reshape x6 -> x1, local copies, waits for them, and re-layouts: 29.6 us -> 7.3 us  [shards(): grad_mixed = grad_mixed[:, :SLOT].astype(jnp.float32).reshape(length, -1)]
    unnamed x1 -> x0, blocking collectives: 21.7 us -> none
    convert_element_type x2 -> x1, local copies, waits for them, and re-layouts: 25.2 us -> 4.22 us  [shards(): activated = jax.nn.silu(attended).astype(jnp.bfloat16)]
    psum x1, waiting for transfers between devices: 17.3 us -> 33.3 us  [shards(): lax.psum(qkv_grad.astype(jnp.bfloat16), 'dp').astype(jnp.float32)]
  transfers between devices with their start and end apart: 5 -> 5, of which waited for: 5 -> 5; matrix products, arithmetic and copies ran while one was open for 3% -> 4% of each run, Pallas kernels for 0% -> 0%
where the time goes in v2:
time: 797 us; the launch traced here: 787 us
  blocking collectives  281 us (35%)
  waiting for transfers between devices  251 us (31%)
  Pallas kernels  66.8 us (8%)
  local copies, waits for them, and re-layouts  65.4 us (8%)
  other arithmetic  59.4 us (7%)
  matrix products  48.4 us (6%)
  between operations  14.4 us (2%)
    psum x4, blocking collectives, norm_backward(): lax.psum((jnp.sum(grad, axis=0), jnp.sum(grad * normed, axis=0)), ('dp',...  162 us
    psum x3, blocking collectives, norm_forward(): lax.psum((jnp.sum(value * weights, axis=0), jnp.sum(value * value * weigh...  120 us
    reduce_scatter x1, waiting for transfers between devices, shards(): lax.psum_scatter(whole[2].astype(jnp.bfloat16), 'fsdp', scatter_dimension...  63.6 us
    reduce_scatter x1, waiting for transfers between devices, shards(): lax.psum_scatter(whole[1].astype(jnp.bfloat16), 'fsdp', scatter_dimension...  63.5 us
    reduce_scatter x1, waiting for transfers between devices, shards(): lax.psum_scatter(whole[3].astype(jnp.bfloat16), 'fsdp', scatter_dimension...  62 us
    psum x1, waiting for transfers between devices, shards(): lax.psum(qkv_grad.astype(jnp.bfloat16), 'dp').astype(jnp.float32)  33.3 us
    pallas_call x1, Pallas kernels, first_call(): pl.pallas_call(functools.partial(first_kernel, dp_size, fs_size), out_sha...  32.5 us
    unnamed x6, waiting for transfers between devices  29.1 us
  transfers between devices with their start and end apart: 5, of which 5 were waited for; matrix products, arithmetic and copies ran while one was open for 4% of the time, Pallas kernels for 0%

profile of v2, /device:TPU:0, one launch (start us, length us, event | category | flops | bytes accessed | tf_op | source)
XLA Modules:
  0.0 787.5 jit_solution(4830409078193117093)
XLA Ops:
  11.5 32.5 %shard_map.280 = (bf16[8,336,768]{2,1,0:T(8,128)(2,1)}, bf16[8,336,256]{2,1,0:T(8,128)(2,1)}, f32[2,112,256]{2,1,0:T(8,128)}, f32[2,208,512]{2,1,0:T(8,128)}, f3...) custom-call(s32[8]{0:T(128)} %class_ref.3, ...), custom_call_target="tpu_custom_call" | custom-call | tf_op jit(solution)/shard_map/pallas_call | solution.py:563
  51.4 11.5 %shard_map.281 = (bf16[8,336,512]{2,1,0:T(8,128)(2,1)}, bf16[8,336,1536]{2,1,0:T(8,128)(2,1)}, f32[8,336,128]{2,1,0:T(8,128)S(1)}) custom-call(s32[8]{0:T(128)S(1)} %copy-done.6, bf16[8,336,768]{2,1,0:T(8,128)(2,1)} %get-tuple-element.31.mixed_ref, f32[2,112,256]{2,1,0:T(8,128)S(1)} %copy-done.5, f32[2,208,512]{2,1,0:T(8,128)S(1)} %copy-done.4, ...), custom_call_target="tpu_custom_call" | custom-call | tf_op jit(solution)/shard_map/pallas_call | solution.py:241
  62.9 4.9 multiply_convert_fusion
  76.1 4.2 convert_element_type.93
  80.3 4.1 multiply_reduce_fusion.8
  84.4 39.3 %all-reduce.7 = (f32[256]{0:T(256)S(1)}, f32[]{:T(128)}, f32[256]{0:T(256)S(1)}) all-reduce(f32[256]{0:T(256)S(1)} %get-tuple-element.99, f32[]{:T(128)} %fusion.14, f32[256]{0:T(256)S(1)} %get-tuple-element.98), channel_id=1, replica_groups=mesh['dp'=4,'fsdp'=8] {'dp','fsdp'}, use_global_device_ids=true, to_apply=%region_1.2 | all-reduce | flops 513 | bytes 4104 | tf_op jit(solution)/shard_map/psum | solution.py:603
  129.7 40.3 %all-reduce.6 = (f32[512]{0:T(512)S(1)}, f32[512]{0:T(512)S(1)}) all-reduce(f32[512]{0:T(512)S(1)} %get-tuple-element.93, f32[512]{0:T(512)S(1)} %get-tuple-element.92), channel_id=1, replica_groups=mesh['dp'=4,'fsdp'=8] {'dp','fsdp'}, use_global_device_ids=true, to_apply=%region_9.10 | all-reduce | flops 1024 | bytes 8192 | tf_op jit(solution)/shard_map/psum | solution.py:603
  170.7 4.2 multiply_convert_fusion.4
  177.3 39.9 %all-reduce.5 = (f32[256]{0:T(256)S(1)}, f32[256]{0:T(256)S(1)}) all-reduce(f32[256]{0:T(256)S(1)} %get-tuple-element.97, f32[256]{0:T(256)S(1)} %get-tuple-element.96), channel_id=1, replica_groups=mesh['dp'=4,'fsdp'=8] {'dp','fsdp'}, use_global_device_ids=true, to_apply=%region_11.12 | all-reduce | flops 512 | bytes 4096 | tf_op jit(solution)/shard_map/psum | solution.py:603
  221.0 40.2 %all-reduce.4 = (f32[256]{0:T(256)S(1)}, f32[256]{0:T(256)S(1)}) all-reduce(f32[256]{0:T(256)S(1)} %multiply_reduce_fusion.4, f32[256]{0:T(256)S(1)} %multiply_reduce_fusion.5), channel_id=1, replica_groups=mesh['dp'=4,'fsdp'=8] {'dp','fsdp'}, use_global_device_ids=true, to_apply=%region_17.18 | all-reduce | flops 512 | bytes 4096 | tf_op jit(solution)/shard_map/psum | solution.py:620
  265.0 6.9 fusion.16
  271.9 39.8 %all-reduce.3 = (f32[512]{0:T(512)S(1)}, f32[512]{0:T(512)S(1)}) all-reduce(f32[512]{0:T(512)S(1)} %get-tuple-element.95, f32[512]{0:T(512)S(1)} %get-tuple-element.94), channel_id=1, replica_groups=mesh['dp'=4,'fsdp'=8] {'dp','fsdp'}, use_global_device_ids=true, to_apply=%region_21.22 | all-reduce | flops 1024 | bytes 8192 | tf_op jit(solution)/shard_map/psum | solution.py:620
  311.8 6.4 multiply_convert_fusion.3
  322.2 5.4 reshape.142
  327.6 40.5 %all-reduce.2 = (f32[256]{0:T(256)S(1)}, f32[256]{0:T(256)S(1)}) all-reduce(f32[256]{0:T(256)S(1)} %get-tuple-element.101, f32[256]{0:T(256)S(1)} %get-tuple-element.100), channel_id=1, replica_groups=mesh['dp'=4,'fsdp'=8] {'dp','fsdp'}, use_global_device_ids=true, to_apply=%region_25.26 | all-reduce | flops 512 | bytes 4096 | tf_op jit(solution)/shard_map/psum | solution.py:620
  368.1 6.2 multiply_convert_fusion.5
  378.7 4.3 reshape.143
  386.5 17.6 %shard_map.282 = (bf16[8,336,768]{2,1,0:T(8,128)(2,1)}, f32[2,112,256]{2,1,0:T(8,128)S(1)}, f32[2,208,512]{2,1,0:T(8,128)S(1)}, f32[2,336,768]{2,1,0:T(8,128)S(1)}) custom-call(s32[8]{0:T(128)S(1)} %copy-done.6, bf16[8,336,768]{2,1,0:T(8,128)(2,1)} %get-tuple-element.31.mixed_ref, bf16[8,336,1536]{2,1,0:T(8,128)(2,1)} %get-tuple-element.40.p_ref, ...), custom_call_target="tpu_custom_call" | custom-call | tf_op jit(solution)/shard_map/pallas_call | solution.py:261
  407.7 5.9 slice_convert_fusion
  413.6 7.3 reshape.144
  422.5 5.2 shard_map.283
  427.7 7.6 fusion
  435.3 41.1 %all-reduce.1 = (f32[768]{0:T(1024)S(1)}, f32[768]{0:T(1024)S(1)}, f32[4,324]{1,0:T(4,128)}) all-reduce(f32[768]{0:T(1024)S(1)} %get-tuple-element.168, f32[768]{0:T(1024)S(1)} %fusion.9, f32[4,324]{1,0:T(4,128)S(1)} %bitcast.69), channel_id=1, replica_groups=mesh['dp'=4,'fsdp'=8] {'dp','fsdp'}, use_global_device_ids=true, to_apply=%region_29.30 | all-reduce | flops 2832 | bytes 22656 | tf_op jit(solution)/shard_map/psum | solution.py:620
  476.4 7.9 %fusion.7 = bf16[2592,768]{1,0:T(8,128)(2,1)S(1)} fusion(f32[2592,768]{1,0:T(8,128)} %reshape.144, f32[768,2592]{0,1:T(8,128)} %get-tuple-element.169, f32[]{:T(128)} %bitcast.17, f32[768]{0:T(1024)S(1)} %get-tuple-element.105, f32[768]{0:T(1024)S(1)} %get-tuple-element.104, f32[768]{0:T(1024)S(1)} %get-tuple-element.103, f32[768]{0:T(1024)S(1)} %get-tuple-element.106, ...), kind=kLoop, calls=%fused_computation.10 | loop fusion | flops 21897216 | bytes 19932292 | tf_op jit(solution)/shard_map/convert_element_type | solution.py:730
  495.9 5.7 fusion.10
  501.6 4.9 convolution_add_fusion.1
  516.8 4.1 copy.50
  521.3 29.0 %reduce-scatter.13.cloned.1.call-done = bf16[32,768]{1,0:T(8,128)(2,1)} async-done(((bf16[256,768]{1,0:T(8,128)(2,1)}), bf16[32,768]{1,0:T(8,128)(2,1)}) %reduce-scatter.13.cloned.1.call-update) | async-done | bytes 49168
  551.9 62.0 %reduce-scatter.11.cloned.1.call-done = bf16[64,256]{1,0:T(8,128)(2,1)} async-done(((bf16[512,256]{1,0:T(8,128)(2,1)}), bf16[64,256]{1,0:T(8,128)(2,1)}) %reduce-scatter.11.cloned.1.call-update) | async-done | bytes 32784 | tf_op jit(solution)/shard_map/reduce_scatter | solution.py:753
  613.9 63.6 %reduce-scatter.9.cloned.1.call-done = bf16[32,512]{1,0:T(8,128)(2,1)} async-done(((bf16[256,512]{1,0:T(8,128)(2,1)}), bf16[32,512]{1,0:T(8,128)(2,1)}) %reduce-scatter.9.cloned.1.call-update) | async-done | bytes 32784 | tf_op jit(solution)/shard_map/reduce_scatter | solution.py:750
  677.5 63.5 %reduce-scatter.7.cloned.1.call-done = bf16[64,256]{1,0:T(8,128)(2,1)} async-done(((bf16[512,256]{1,0:T(8,128)(2,1)}), bf16[64,256]{1,0:T(8,128)(2,1)}) %reduce-scatter.7.cloned.1.call-update) | async-done | bytes 32784 | tf_op jit(solution)/shard_map/reduce_scatter | solution.py:747
  741.6 33.3 %all-reduce.11.cloned.1.call-done = (bf16[32,768]{0,1:T(8,128)(2,1)}, bf16[64,256]{1,0:T(8,128)(2,1)}, bf16[32,512]{1,0:T(8,128)(2,1)}, bf16[64,256]{1,0:T(8,128)(2,1)}) async-done(((bf16[32,768]{0,1:T(8,128)(2,1)}, bf16[64,256]{1,0:T(8,128)(2,1)}, bf16[32,512]{1,0:T(8,128)(2,1)}, bf16[64,256]{1,0:T(8,128)(2,1)}), (bf16[32,768]{0,1:T(8,128)(2,1)}, bf16[64,256]{1,0:T(8,128)(2,1)}, bf16[32,512]{1,0:T(8,128)(2,1)}, ...) | async-done | bytes 147472 | tf_op jit(solution)/shard_map/psum | solution.py:738
  (136 shorter events, 83.7 us)
Async XLA Ops:
  7.2 543.1 %reduce-scatter.13.cloned.1.call-start = ((), (), s32[]{:S(2)}) async-start(), calls=%async_computation.7 | async-start | bytes 442368
  10.5 37.3 %copy-start.6 = (s32[8]{0:T(128)S(1)}, s32[8]{0:T(128)}, u32[]{:S(2)}) copy-start(s32[8]{0:T(128)} %class_ref.3) | copy-start | bytes 100
  10.8 357.4 %copy-start.8 = (bf16[2592,256]{1,0:T(8,128)(2,1)}, bf16[2592,256]{1,0:T(8,128)(2,1)S(1)}, u32[]{:S(2)}) copy-start(bf16[2592,256]{1,0:T(8,128)(2,1)S(1)} %reshape.128) | copy-start | bytes 3981316
  47.7 1.6 copy-start.1
  49.3 1.2 copy-start.4
  62.9 4.9 copy-start.13
  67.8 3.2 copy-start.20
  76.1 4.2 copy-start.27
  124.4 2.4 copy-start.26
  126.8 3.0 copy-start.25
  170.7 4.2 copy-start.28
  174.9 2.4 copy-start.17
  261.1 3.9 copy-start.29
  265.0 6.9 copy-start.22
  311.8 7.9 %copy-start.11 = (f32[2592,256]{1,0:T(8,128)S(1)}, f32[2592,256]{1,0:T(8,128)}, u32[]{:S(2)}) copy-start(f32[2592,256]{1,0:T(8,128)} %reshape.141) | copy-start | bytes 7962628
  311.8 7.9 %copy-start.14 = (f32[2592,256]{1,0:T(8,128)S(1)}, f32[2592,256]{1,0:T(8,128)}, u32[]{:S(2)}) copy-start(f32[2592,256]{1,0:T(8,128)} %get-tuple-element.163) | copy-start | bytes 7962628
  318.2 1.5 copy-start.19
  368.1 7.2 copy-start.21
  404.2 3.5 copy-start.2
  413.6 7.3 copy-start
  413.6 14.1 %copy-start.23 = (bf16[8,32,768]{2,1,0:T(8,128)(2,1)S(1)}, bf16[8,32,768]{2,1,0:T(8,128)(2,1)}, u32[]{:S(2)}) copy-start(bf16[8,32,768]{2,1,0:T(8,128)(2,1)} %get-tuple-element.43) | copy-start | bytes 1179652
  420.9 1.6 copy-start.3
  422.5 5.2 copy-start.9
  476.4 9.8 %copy-start.10 = (bf16[2592,256]{1,0:T(8,128)(2,1)S(1)}, bf16[2592,256]{1,0:T(8,128)(2,1)}, u32[]{:S(2)}) copy-start(bf16[2592,256]{1,0:T(8,128)(2,1)} %copy-done.8) | copy-start | bytes 3981316
  484.3 1.9 copy-start.7
  486.2 2.5 copy-start.18
  488.7 125.2 %reduce-scatter.11.cloned.1.call-start = ((), (), s32[]{:S(2)}) async-start(), calls=%async_computation.6 | async-start | bytes 294912 | tf_op jit(solution)/shard_map/reduce_scatter | solution.py:753
  491.7 185.8 %reduce-scatter.9.cloned.1.call-start = ((), (), s32[]{:S(2)}) async-start(), calls=%async_computation.5 | async-start | bytes 294912 | tf_op jit(solution)/shard_map/reduce_scatter | solution.py:750
  495.6 245.4 %reduce-scatter.7.cloned.1.call-start = ((), (), s32[]{:S(2)}) async-start(), calls=%async_computation.4 | async-start | bytes 294912 | tf_op jit(solution)/shard_map/reduce_scatter | solution.py:747
  495.8 5.8 copy-start.12
  501.6 273.3 %all-reduce.11.cloned.1.call-start = ((), (), s32[]{:S(2)}) async-start(), calls=%async_computation.8 | async-start | bytes 589824 | tf_op jit(solution)/shard_map/psum | solution.py:738
  510.1 5.1 copy-start.15
  (3 other events, 3.1 us)
Sparse Core Ops, SparseCore 0:
  488.8 61.4 reduce-scatter.12
  553.6 60.2 reduce-scatter.10
  617.2 60.2 reduce-scatter.8
  680.7 60.2 reduce-scatter.6
  743.3 31.5 all-reduce.10

commit v3 on v2

--- a/solution.py
+++ b/solution.py
@@ -272,20 +272,6 @@
     )(classes, mixed, probs, shares, grad, attended)
 
 
-def table_kernel(off_ref, acc0, acc1, acc2, out_ref):
-    out_ref[...] = table_sums(off_ref, (acc0, acc1, acc2))
-
-
-def table_call(offset_table, accs):
-    return pl.pallas_call(
-        table_kernel,
-        out_shape=jax.ShapeDtypeStruct((HEADS, 384), jnp.float32),
-        in_specs=[VMEM] * 4,
-        out_specs=VMEM,
-        compiler_params=pltpu.CompilerParams(vmem_limit_bytes=48 * 2**20),
-    )(offset_table, *accs)
-
-
 MESH = pl.DeviceIdType.MESH
 ANY = pl.BlockSpec(memory_space=pl.ANY)
 SMEM = pl.BlockSpec(memory_space=pltpu.SMEM)
@@ -421,6 +407,20 @@
     return jnp.concatenate(parts, axis=1)
 
 
+def by_columns(ref, value):
+    for k in range(ref.shape[0]):
+        ref[k] = value[:, 128 * k : 128 * k + 128]
+
+
+def take_image(ref, image, images):
+    return jnp.concatenate([ref[k, pl.ds(image, SLOT, stride=images), :] for k in range(ref.shape[0])], axis=1)
+
+
+def put_image(ref, image, images, value):
+    for k in range(ref.shape[0]):
+        ref[k, pl.ds(image, SLOT, stride=images), :] = value[:SLOT, 128 * k : 128 * k + 128]
+
+
 def limits_of(kind):
     return jnp.where(kind == 0, (GRID - 8) ** 2, jnp.where(kind == 1, (GRID - 4) ** 2, SLOT))
 
@@ -439,12 +439,12 @@
     class_ref, x_ref, off_ref, table_ref = refs[:4]
     shards, vectors = refs[4:8], refs[8:16]
     mixed_out, xs_out, bias_out, weight_out, vec_out = refs[16], refs[17], refs[18:21], refs[21:25], refs[25]
-    xs, z, mixed, index = refs[26:30]
-    bias, weights = refs[30:33], refs[33:37]
-    vbuf, stat = refs[37:39]
-    send, recv, send2, recv2, local = refs[39:44]
+    xs, z, mixed, index, wide = refs[26:31]
+    bias, weights = refs[31:34], refs[34:38]
+    vbuf, stat = refs[38:40]
+    send, recv, send2, recv2, local = refs[40:45]
     place = Place(dp_size, fs_size)
-    images = x_ref.shape[0]
+    images = xs.shape[0]
 
     for k in range(4):
         own = shards[k][...]
@@ -456,14 +456,15 @@
     )
     place.greet()
 
-    def load(image, count):
+    by_columns(wide, x_ref[...].astype(jnp.float32))
+    count = jnp.int32(0)
+    for image in range(images):
         limit = limits_of(class_ref[image])
-        row = lax.broadcasted_iota(jnp.int32, (SLOT, 1), 0)
-        value = jnp.where(row < limit, x_ref[image].astype(jnp.float32), 0.0)
+        row = lax.broadcasted_iota(jnp.int32, (SLOT, xs.shape[2]), 0)
+        value = jnp.where(row < limit, take_image(wide, image, images), 0.0)
         xs[image] = pad_rows(value, ROWS).astype(jnp.bfloat16)
-        return count + limit
-
-    count = lax.fori_loop(0, images, load, 0)
+        count = count + limit
+
     flat = xs[...].reshape(images * ROWS, xs.shape[2])
     gram = dot_tn(flat, flat)
     total_x = dot_nn(jnp.ones((8, images * ROWS), jnp.bfloat16), flat)
@@ -555,7 +556,7 @@
 
 
 def first_call(dp_size, fs_size, classes, inputs, offset_table, bias_table, weights, vectors):
-    images, model = inputs.shape[0], inputs.shape[2]
+    images, model = classes.shape[0], inputs.shape[1]
     vectors = [v.reshape(1, -1) for v in vectors]
     shapes = [(fs_size,) + w.shape for w in weights]
     biases = [(2, r, 2 * l) for _, _, r, l in PARTS]
@@ -576,6 +577,7 @@
             pltpu.VMEM((images, ROWS, 768), f32),
             pltpu.VMEM((images, ROWS, 768), bf),
             pltpu.VMEM((ROWS, 384), jnp.int32),
+            pltpu.VMEM((model // 128, inputs.shape[0], 128), f32),
         ]
         + [pltpu.VMEM(s, f32) for s in biases]
         + [pltpu.VMEM(s, bf) for s in shapes]
@@ -594,50 +596,550 @@
     )(classes, inputs, offset_table, bias_table, *weights, *vectors)
 
 
-def silu_slope(value):
-    sigma = jax.nn.sigmoid(value)
+def total_rows(value):
+    return jnp.sum(value, axis=0, keepdims=True)
+
+
+def sigma_of(value):
+    return 0.5 * jnp.tanh(0.5 * value) + 0.5
+
+
+def slope_of(value):
+    sigma = sigma_of(value)
     return sigma * (1.0 + value * (1.0 - sigma))
 
 
-def norm_forward(value, weights, gain, shift):
-    sums = lax.psum(
-        (
-            jnp.sum(value * weights, axis=0),
-            jnp.sum(value * value * weights, axis=0),
-            jnp.sum(weights),
+def norm_parts(sums, squares, total, gain, shift):
+    center = sums / total
+    scale = lax.rsqrt(squares / total - center * center + EPS)
+    return center, scale, scale * gain, shift - center * scale * gain
+
+
+def back_parts(grad_sum, grad_z, total, gain, center, scale):
+    gain_grad = scale * (grad_z - center * grad_sum)
+    alpha = scale * gain
+    slant = alpha * scale * gain_grad / total
+    level = alpha * (grad_sum - center * scale * gain_grad) / total
+    return gain_grad, alpha, slant, level
+
+
+def outer(column, row):
+    left = jnp.concatenate([column, jnp.zeros((7, column.shape[1]), jnp.float32)], axis=0)
+    right = jnp.concatenate([row, jnp.zeros((7, row.shape[1]), jnp.float32)], axis=0)
+    left_high, left_low = split_low(left)
+    right_high, right_low = split_low(right)
+    return dot_tn(left_high, right_high) + dot_tn(left_high, right_low) + dot_tn(left_low, right_high)
+
+
+def middle_kernel(dp_size, fs_size, group, *refs):
+    class_ref, att_in, xs_in, cot_in = refs[:4]
+    weight_in, vec_ref = refs[4:7], refs[7]
+    out_out, gatt_out, gm_out, grad_out, vec_out = refs[8], refs[9], refs[10], refs[11:14], refs[14]
+    att, xs, cot, wo_buf, wu_buf, wd_buf = refs[15:21]
+    gs, act, slope_att, zo, low, zu, hid, slope_up, zd, dzd, gu, gm, dzo, out, gatt, wide = refs[21:37]
+    stat_o, stat_u, stat_d, stat_bu, stat_bo = refs[37:42]
+    send, recv, local = refs[42:45]
+    place = Place(dp_size, fs_size)
+    images = att.shape[0]
+    chunks = images // group
+    size = group * ROWS
+    f32, bf = jnp.float32, jnp.bfloat16
+
+    def copy(source, target, at):
+        return pltpu.make_async_copy(source, target, local.at[at])
+
+    loads = [
+        copy(weight_in[0], wo_buf, 0),
+        copy(xs_in, xs, 1),
+        copy(cot_in, cot, 2),
+        copy(weight_in[1], wu_buf, 3),
+        copy(weight_in[2], wd_buf, 4),
+    ]
+    loads[0].start()
+
+    def att_copy(k):
+        part = pl.ds(k * group, group)
+        return copy(att_in.at[part], att.at[part], 8 + k)
+
+    for k in range(chunks):
+        att_copy(k).start()
+    for load in loads[1:]:
+        load.start()
+    place.greet()
+
+    def get(ref, k):
+        return ref[pl.ds(k * group, group)].reshape(size, ref.shape[2])
+
+    def put(ref, k, value):
+        ref[pl.ds(k * group, group)] = value.astype(ref.dtype).reshape(group, ROWS, ref.shape[2])
+
+    def kept(k, width):
+        row = lax.broadcasted_iota(jnp.int32, (ROWS, width), 0)
+        return jnp.concatenate([row < limits_of(class_ref[k * group + j]) for j in range(group)], axis=0)
+
+    def over(body, carry):
+        return lax.fori_loop(0, chunks, body, carry)
+
+    def zero(width):
+        return jnp.zeros((1, width), f32)
+
+    model = xs.shape[2]
+    hidden = zu.shape[2]
+    total = vec_ref[10:11, :1]
+    out_gain, out_shift = vec_ref[2:3, :model], vec_ref[3:4, :model]
+    up_gain, up_shift = vec_ref[4:5, :hidden], vec_ref[5:6, :hidden]
+    down_gain, down_shift = vec_ref[6:7, :model], vec_ref[7:8, :model]
+
+    loads[0].wait()
+    wo = flat_weight(wo_buf)
+
+    def step_out(k, carry):
+        att_copy(k).wait()
+        value = get(att, k).astype(f32)
+        active = (value * sigma_of(value)).astype(bf)
+        put(act, k, active)
+        z = dot_nn(active, wo)
+        put(zo, k, z)
+        return carry[0] + total_rows(z), carry[1] + total_rows(z * z)
+
+    sums = over(step_out, (zero(model), zero(model)))
+    place.meet()
+    place.spread(stat_o, jnp.concatenate(sums, axis=0), send.at[0], recv.at[0])
+    for load in loads[1:]:
+        load.wait()
+
+    def fill_out(k, _):
+        put(slope_att, k, slope_of(get(att, k).astype(f32)))
+        return 0
+
+    over(fill_out, 0)
+    by_columns(wide, cot[...].astype(f32))
+    grad_sum = zero(model)
+    for image in range(images):
+        row = lax.broadcasted_iota(jnp.int32, (SLOT, model), 0)
+        value = jnp.where(row < limits_of(class_ref[image]), take_image(wide, image, images), 0.0)
+        gs[image] = pad_rows(value, ROWS).astype(bf)
+        grad_sum = grad_sum + total_rows(value)
+    wu, wd = flat_weight(wu_buf), flat_weight(wd_buf)
+    got = place.collect(stat_o, recv.at[0])
+    center_o, scale_o, a_o, b_o = norm_parts(got[0:1], got[1:2], total, out_gain, out_shift)
+
+    def middle_of(k):
+        return get(xs, k).astype(f32) + get(zo, k) * a_o + b_o
+
+    def step_up(k, carry):
+        lower = jnp.where(kept(k, model), middle_of(k), 0.0).astype(bf)
+        put(low, k, lower)
+        z = dot_nn(lower, wu)
+        put(zu, k, z)
+        return carry[0] + total_rows(z), carry[1] + total_rows(z * z)
+
+    sums = over(step_up, (zero(hidden), zero(hidden)))
+    place.spread(stat_u, jnp.concatenate(sums, axis=0), send.at[1], recv.at[1])
+    low_flat = low[...].reshape(images * ROWS, model)
+    low_gram = dot_tn(low_flat, low_flat)
+    low_sum = dot_nn(jnp.ones((8, images * ROWS), bf), low_flat)[:1]
+    got = place.collect(stat_u, recv.at[1])
+    center_u, scale_u, a_u, b_u = norm_parts(got[0:1], got[1:2], total, up_gain, up_shift)
+
+    def step_down(k, carry):
+        value = get(zu, k) * a_u + b_u
+        active = jnp.where(kept(k, hidden), value * sigma_of(value), 0.0).astype(bf)
+        put(hid, k, active)
+        z = dot_nn(active, wd)
+        put(zd, k, z)
+        return (
+            carry[0] + total_rows(z),
+            carry[1] + total_rows(z * z),
+            carry[2] + total_rows(z * get(gs, k).astype(f32)),
+        )
+
+    sums = over(step_down, (zero(model), zero(model), zero(model)))
+    place.spread(stat_d, jnp.concatenate(sums + (grad_sum,), axis=0), send.at[2], recv.at[2])
+
+    def fill_down(k, _):
+        put(slope_up, k, slope_of(get(zu, k) * a_u + b_u))
+        return 0
+
+    over(fill_down, 0)
+    got = place.collect(stat_d, recv.at[2])
+    center_d, scale_d, a_d, b_d = norm_parts(got[0:1], got[1:2], total, down_gain, down_shift)
+    down_shift_grad = got[3:4]
+    down_gain_grad, alpha, slant, level = back_parts(got[3:4], got[2:3], total, down_gain, center_d, scale_d)
+
+    def step_back_down(k, carry):
+        dz = get(gs, k).astype(f32) * alpha - get(zd, k) * slant - jnp.where(kept(k, model), level, 0.0)
+        dz = dz.astype(bf)
+        put(dzd, k, dz)
+        grad = dot_nt(dz, wd) * get(slope_up, k).astype(f32)
+        put(gu, k, grad)
+        return carry[0] + total_rows(grad), carry[1] + total_rows(grad * get(zu, k))
+
+    sums = over(step_back_down, (zero(hidden), zero(hidden)))
+    place.spread(stat_bu, jnp.concatenate(sums, axis=0), send.at[3], recv.at[3])
+
+    def fill_back_down(k, carry):
+        grad = get(gu, k)
+        carry = carry + dot_tn(get(low, k), grad.astype(bf))
+        put(gm, k, get(gs, k).astype(f32) + dot_nt((grad * a_u).astype(bf), wu))
+        return carry
+
+    up_raw = over(fill_back_down, jnp.zeros((model, hidden), f32))
+    for image in range(images):
+        row = lax.broadcasted_iota(jnp.int32, (ROWS, model), 0)
+        value = xs[image].astype(f32) + zo[image] * a_o + zd[image] * a_d + (b_o + b_d)
+        value = jnp.where(row < limits_of(class_ref[image]), value, 0.0)
+        put_image(wide, image, images, value)
+    for k in range(wide.shape[0]):
+        out[:, 128 * k : 128 * k + 128] = wide[k].astype(bf)
+    out_copy = copy(out, out_out, 5)
+    out_copy.start()
+    down_grad = dot_tn(hid[...].reshape(images * ROWS, hidden), dzd[...].reshape(images * ROWS, model))
+    grad_out[2][...] = down_grad.reshape(grad_out[2].shape).astype(bf)
+    got = place.collect(stat_bu, recv.at[3])
+    up_shift_grad = got[0:1]
+    up_gain_grad, alpha_u, slant_u, level_u = back_parts(got[0:1], got[1:2], total, up_gain, center_u, scale_u)
+    mix = dot_nt((wu.astype(f32) * slant_u).astype(bf), wu).astype(bf)
+    high, rest = split_low(jnp.broadcast_to(level_u, (8, hidden)))
+    lift = (dot_nt(high, wu) + dot_nt(rest, wu))[:1]
+
+    def step_back_up(k, carry):
+        grad = get(gm, k) - dot_nn(get(low, k), mix) - jnp.where(kept(k, model), lift, 0.0)
+        put(gm, k, grad)
+        part = pl.ds(k * group, group)
+        copy(gm.at[part], gm_out.at[part], 8 + chunks + k).start()
+        return carry[0] + total_rows(grad), carry[1] + total_rows(grad * get(zo, k))
+
+    sums = over(step_back_up, (zero(model), zero(model)))
+    place.spread(stat_bo, jnp.concatenate(sums, axis=0), send.at[4], recv.at[4])
+    up_grad = up_raw * alpha_u - precise(low_gram, wu) * slant_u - outer(low_sum, level_u)
+    grad_out[1][...] = up_grad.reshape(grad_out[1].shape).astype(bf)
+    got = place.collect(stat_bo, recv.at[4])
+    out_shift_grad = got[0:1]
+    out_gain_grad, alpha_o, slant_o, level_o = back_parts(got[0:1], got[1:2], total, out_gain, center_o, scale_o)
+
+    def step_back_out(k, _):
+        dz = get(gm, k) * alpha_o - get(zo, k) * slant_o - jnp.where(kept(k, model), level_o, 0.0)
+        dz = dz.astype(bf)
+        put(dzo, k, dz)
+        put(gatt, k, dot_nt(dz, wo) * get(slope_att, k).astype(f32))
+        part = pl.ds(k * group, group)
+        copy(gatt.at[part], gatt_out.at[part], 8 + 2 * chunks + k).start()
+        return 0
+
+    over(step_back_out, 0)
+    out_grad = dot_tn(act[...].reshape(images * ROWS, act.shape[2]), dzo[...].reshape(images * ROWS, model))
+    grad_out[0][...] = out_grad.reshape(grad_out[0].shape).astype(bf)
+    vec_out[...] = jnp.concatenate(
+        [
+            pad_lanes(v, hidden)
+            for v in (
+                out_gain_grad,
+                out_shift_grad,
+                up_gain_grad,
+                up_shift_grad,
+                down_gain_grad,
+                down_shift_grad,
+                zero(hidden),
+                zero(hidden),
+            )
+        ],
+        axis=0,
+    )
+    for k, stat in enumerate((stat_o, stat_u, stat_d, stat_bu, stat_bo)):
+        place.settle(stat, send.at[k])
+
+    def finish(k, _):
+        part = pl.ds(k * group, group)
+        copy(gm.at[part], gm_out.at[part], 8 + chunks + k).wait()
+        copy(gatt.at[part], gatt_out.at[part], 8 + 2 * chunks + k).wait()
+        return 0
+
+    over(finish, 0)
+    out_copy.wait()
+
+
+def middle_call(dp_size, fs_size, classes, attended, xs, cotangent, weights, vec):
+    images, model, feature, hidden = xs.shape[0], xs.shape[2], attended.shape[2], weights[1].shape[2]
+    group = 2 if images % 2 == 0 else 1
+    chunks = images // group
+    devices = dp_size * fs_size
+    bf, f32 = jnp.bfloat16, jnp.float32
+
+    def rows(width, kind):
+        return pltpu.VMEM((images, ROWS, width), kind)
+
+    return pl.pallas_call(
+        functools.partial(middle_kernel, dp_size, fs_size, group),
+        out_shape=[
+            jax.ShapeDtypeStruct(cotangent.shape, bf),
+            jax.ShapeDtypeStruct((images, ROWS, feature), bf),
+            jax.ShapeDtypeStruct((images, ROWS, model), f32),
+        ]
+        + [jax.ShapeDtypeStruct(w.shape, bf) for w in weights]
+        + [jax.ShapeDtypeStruct((8, hidden), f32)],
+        in_specs=[SMEM] + [ANY] * 6 + [VMEM],
+        out_specs=[ANY] * 3 + [VMEM] * 4,
+        scratch_shapes=[
+            rows(feature, bf),
+            rows(model, bf),
+            pltpu.VMEM(cotangent.shape, bf),
+        ]
+        + [pltpu.VMEM(w.shape, bf) for w in weights]
+        + [
+            rows(model, bf),
+            rows(feature, bf),
+            rows(feature, bf),
+            rows(model, f32),
+            rows(model, bf),
+            rows(hidden, f32),
+            rows(hidden, bf),
+            rows(hidden, bf),
+            rows(model, f32),
+            rows(model, bf),
+            rows(hidden, f32),
+            rows(model, f32),
+            rows(model, bf),
+            pltpu.VMEM(cotangent.shape, bf),
+            rows(feature, bf),
+            pltpu.VMEM((model // 128, cotangent.shape[0], 128), f32),
+            pltpu.VMEM((devices, 2, model), f32),
+            pltpu.VMEM((devices, 2, hidden), f32),
+            pltpu.VMEM((devices, 4, model), f32),
+            pltpu.VMEM((devices, 2, hidden), f32),
+            pltpu.VMEM((devices, 2, model), f32),
+            pltpu.SemaphoreType.DMA((5,)),
+            pltpu.SemaphoreType.DMA((5,)),
+            pltpu.SemaphoreType.DMA((8 + 3 * chunks,)),
+        ],
+        compiler_params=pltpu.CompilerParams(
+            collective_id=1, has_side_effects=True, vmem_limit_bytes=58 * 2**20
         ),
-        ("dp", "fsdp"),
+    )(classes, attended, xs, cotangent, *weights, vec)
+
+
+class Reduce:
+    def __init__(self, place, full, first, half, second, third, send, recv):
+        self.place, self.full, self.first, self.half = place, full, first, half
+        self.second, self.third, self.send, self.recv = second, third, send, recv
+        self.width = half.shape[2]
+
+    def by_core(self, body):
+        for core in range(2):
+            pl.when(self.place.core == core)(functools.partial(body, core))
+
+    def swap(self):
+        def body(core):
+            part = self.full.at[:, :, pl.ds((1 - core) * self.width, self.width)]
+            push(part, self.first, self.send.at[0], self.recv.at[0], self.place.partner)
+
+        self.by_core(body)
+
+    def scatter(self):
+        place = self.place
+        await_bytes(self.first, self.recv.at[0])
+
+        def body(core):
+            own = self.full[:, :, core * self.width : (core + 1) * self.width].astype(jnp.float32)
+            self.half[...] = (own + self.first[...].astype(jnp.float32)).astype(jnp.bfloat16)
+
+        self.by_core(body)
+        self.second[place.fs] = self.half[place.fs]
+
+        def start(step, _):
+            target = lax.rem(place.fs + step, place.fs_size)
+            push(self.half.at[target], self.second.at[place.fs], self.send.at[1], self.recv.at[1], (place.dp, target))
+            return 0
+
+        lax.fori_loop(1, place.fs_size, start, 0)
+
+    def share(self):
+        place = self.place
+        await_bytes(self.second.at[pl.ds(0, place.fs_size - 1)], self.recv.at[1])
+        total = jnp.sum(self.second[...].astype(jnp.float32), axis=0)
+        self.third[place.dp] = total.astype(jnp.bfloat16)
+
+        def start(step, _):
+            target = lax.rem(place.dp + step, place.dp_size)
+            push(self.third.at[place.dp], self.third.at[place.dp], self.send.at[2], self.recv.at[2], (target, place.fs))
+            return 0
+
+        lax.fori_loop(1, place.dp_size, start, 0)
+
+    def result(self):
+        place = self.place
+        await_bytes(self.third.at[pl.ds(0, place.dp_size - 1)], self.recv.at[2])
+        parts = []
+        for core in range(2):
+            parts.append(sum(self.third[k].astype(jnp.float32) for k in range(core, place.dp_size, 2)))
+        return jnp.concatenate(parts, axis=1)
+
+    def settle(self):
+        place = self.place
+        await_bytes(self.first, self.send.at[0])
+        await_bytes(self.second.at[pl.ds(0, place.fs_size - 1)], self.send.at[1])
+        await_bytes(self.third.at[pl.ds(0, place.dp_size - 1)], self.send.at[2])
+
+
+def last_kernel(dp_size, fs_size, group, *refs):
+    class_ref, xs_in, gmix_in, gm_in, wq_in, off_in = refs[:6]
+    acc_in, grad_in, vec_ref = refs[6:9], refs[9:12], refs[12]
+    ig_out, table_out, own_out, vec_out = refs[13], refs[14], refs[15:19], refs[19]
+    xs, gmix, gm, wq_buf, off, ig, res = refs[20:27]
+    acc, full = refs[27:30], refs[30:34]
+    steps = [refs[34 + 4 * k : 38 + 4 * k] for k in range(4)]
+    stat, stat_t = refs[50:52]
+    send, recv, local, send_r, recv_r = refs[52:57]
+    place = Place(dp_size, fs_size)
+    images = xs.shape[0]
+    chunks = images // group
+    size = group * ROWS
+    f32, bf = jnp.float32, jnp.bfloat16
+    model, width = xs.shape[2], gmix.shape[2]
+
+    def copy(source, target, at):
+        return pltpu.make_async_copy(source, target, local.at[at])
+
+    first_loads = [copy(xs_in, xs, 0), copy(gmix_in, gmix, 1), copy(wq_in, wq_buf, 2)]
+    grad_loads = [copy(grad_in[k], full[1 + k], 3 + k) for k in range(3)]
+    late_loads = [copy(off_in, off, 6)] + [copy(acc_in[k], acc[k], 7 + k) for k in range(3)] + [copy(gm_in, gm, 10)]
+    for load in first_loads + grad_loads + late_loads:
+        load.start()
+    place.greet()
+    reduces = [
+        Reduce(place, full[k], *steps[k], send_r.at[k], recv_r.at[k]) for k in range(4)
+    ]
+
+    def get(ref, k):
+        return ref[pl.ds(k * group, group)].reshape(size, ref.shape[2])
+
+    def put(ref, k, value):
+        ref[pl.ds(k * group, group)] = value.astype(ref.dtype).reshape(group, ROWS, ref.shape[2])
+
+    def kept(k, lanes):
+        row = lax.broadcasted_iota(jnp.int32, (ROWS, lanes), 0)
+        return jnp.concatenate([row < limits_of(class_ref[k * group + j]) for j in range(group)], axis=0)
+
+    total = vec_ref[10:11, :1]
+    gain, scale, center = vec_ref[0:1, :], vec_ref[8:9, :], vec_ref[9:10, :]
+    for load in first_loads:
+        load.wait()
+    weight = flat_weight(wq_buf)
+    weight_f = weight.astype(f32)
+    xs_flat = xs[...].reshape(images * ROWS, model)
+    gmix_flat = gmix[...].reshape(images * ROWS, width)
+    raw = dot_tn(xs_flat, gmix_flat)
+    ones = jnp.ones((8, images * ROWS), bf)
+    grad_sum = dot_nn(ones, gmix_flat)[:1]
+    grad_z = total_rows(raw * weight_f)
+    place.meet()
+    place.spread(stat, jnp.concatenate([grad_sum, grad_z], axis=0), send.at[0], recv.at[0])
+    for load in grad_loads:
+        load.wait()
+    for k in range(1, 4):
+        reduces[k].swap()
+    alpha = scale * gain
+    gram = dot_tn(xs_flat, xs_flat)
+    x_sum = dot_nn(ones, xs_flat)[:1]
+
+    def product(k, _):
+        put(ig, k, dot_nt((get(gmix, k).astype(f32) * alpha).astype(bf), weight))
+        return 0
+
+    lax.fori_loop(0, chunks, product, 0)
+    for k in range(1, 4):
+        reduces[k].scatter()
+    for load in late_loads:
+        load.wait()
+    place.spread(stat_t, table_sums(off, acc), send.at[1], recv.at[1])
+
+    got = place.collect(stat, recv.at[0])
+    gain_grad, alpha, slant, level = back_parts(got[0:1], got[1:2], total, gain, center, scale)
+    own = raw * alpha - precise(gram, weight) * slant - outer(x_sum, level)
+    full[0][...] = restore(own).reshape(full[0].shape).astype(bf)
+    reduces[0].swap()
+    mix = dot_nt((weight_f * slant).astype(bf), weight).astype(bf)
+    high, rest = split_low(jnp.broadcast_to(level, (8, width)))
+    lift = (dot_nt(high, weight) + dot_nt(rest, weight))[:1]
+    vec_out[...] = jnp.concatenate(
+        [restore(gain_grad), restore(got[0:1]), jnp.zeros((6, width), f32)], axis=0
     )
-    total = sums[2]
-    center = sums[0] / total
-    square = sums[1] / total
-    scale = lax.rsqrt(square - center * center + EPS)
-    normed = (value - center) * scale
-    return (normed * gain.astype(jnp.float32) + shift.astype(jnp.float32), normed, scale, total)
-
-
-def norm_backward(grad, normed, scale, total, gain, weights):
-    sums = lax.psum((jnp.sum(grad, axis=0), jnp.sum(grad * normed, axis=0)), ("dp", "fsdp"))
-    shift_grad = sums[0]
-    gain_grad = sums[1]
-    gain_f = gain.astype(jnp.float32)
-    inner = gain_f * (shift_grad + normed * gain_grad) / total
-    return (scale * (grad * gain_f - weights * inner), gain_grad, shift_grad)
-
-
-def attention_scores(query, keys, bias, keep):
-    dots = jnp.einsum("iqhk,iphk->ihqp", query, keys, preferred_element_type=jnp.float32)
-    scores = dots * KEY ** (-0.5) + bias
-    return jnp.where(keep[:, None, None, :] > 0, scores, -1e30)
-
-
-def left_product(left, right):
-    return jnp.einsum("na,nb->ab", left, right, preferred_element_type=jnp.float32)
-
-
-def right_product(left, right):
-    return jnp.einsum("nb,ab->na", left, right, preferred_element_type=jnp.float32)
-
+
+    def result(k):
+        value = get(gm, k) + get(ig, k) - dot_nn(get(xs, k), mix) - jnp.where(kept(k, model), lift, 0.0)
+        for j in range(group):
+            put_image(res, k * group + j, images, value[j * ROWS : (j + 1) * ROWS])
+
+    reduces[0].scatter()
+    for k in range(chunks):
+        result(k)
+    res_copies = [copy(res.at[k], ig_out.at[:, pl.ds(128 * k, 128)], 11 + k) for k in range(model // 128)]
+    for res_copy in res_copies:
+        res_copy.start()
+    for k in range(1, 4):
+        reduces[k].share()
+    table_out[...] = place.collect(stat_t, recv.at[1])
+    reduces[0].share()
+    for k in (1, 2, 3, 0):
+        own_out[k][...] = reduces[k].result()
+    for k in range(4):
+        reduces[k].settle()
+    place.settle(stat, send.at[0])
+    place.settle(stat_t, send.at[1])
+    for res_copy in res_copies:
+        res_copy.wait()
+
+
+def last_call(dp_size, fs_size, classes, xs, gmix, gm, wq, offset_table, accs, grads, vec):
+    images, model, width = xs.shape[0], xs.shape[2], gmix.shape[2]
+    group = 2 if images % 2 == 0 else 1
+    devices = dp_size * fs_size
+    bf, f32 = jnp.bfloat16, jnp.float32
+    shapes = [wq.shape] + [g.shape for g in grads]
+    steps = []
+    for s in shapes:
+        half = s[2] // 2
+        steps += [
+            pltpu.VMEM((fs_size, s[1], half), bf),
+            pltpu.VMEM((fs_size, s[1], half), bf),
+            pltpu.VMEM((fs_size, s[1], half), bf),
+            pltpu.VMEM((dp_size, s[1], half), bf),
+        ]
+    order = []
+    for k in range(4):
+        order += [steps[4 * k], steps[4 * k + 1], steps[4 * k + 2], steps[4 * k + 3]]
+    return pl.pallas_call(
+        functools.partial(last_kernel, dp_size, fs_size, group),
+        out_shape=[jax.ShapeDtypeStruct((SLOT * images, model), f32), jax.ShapeDtypeStruct((HEADS, 384), f32)]
+        + [jax.ShapeDtypeStruct(s[1:], f32) for s in shapes]
+        + [jax.ShapeDtypeStruct((8, width), f32)],
+        in_specs=[SMEM] + [ANY] * 11 + [VMEM],
+        out_specs=[ANY] + [VMEM] * 6,
+        scratch_shapes=[
+            pltpu.VMEM(xs.shape, bf),
+            pltpu.VMEM(gmix.shape, bf),
+            pltpu.VMEM(gm.shape, f32),
+            pltpu.VMEM(wq.shape, bf),
+            pltpu.VMEM(offset_table.shape, jnp.int32),
+            pltpu.VMEM(gm.shape, f32),
+            pltpu.VMEM((model // 128, SLOT * images, 128), f32),
+        ]
+        + [pltpu.VMEM(a.shape, f32) for a in accs]
+        + [pltpu.VMEM(s, bf) for s in shapes]
+        + order
+        + [
+            pltpu.VMEM((devices, 2, width), f32),
+            pltpu.VMEM((devices, HEADS, 384), f32),
+            pltpu.SemaphoreType.DMA((2,)),
+            pltpu.SemaphoreType.DMA((2,)),
+            pltpu.SemaphoreType.DMA((11 + model // 128,)),
+            pltpu.SemaphoreType.DMA((4, 3)),
+            pltpu.SemaphoreType.DMA((4, 3)),
+        ],
+        compiler_params=pltpu.CompilerParams(
+            collective_id=2, has_side_effects=True, vmem_limit_bytes=56 * 2**20
+        ),
+    )(classes, xs, gmix, gm, wq, offset_table, *accs, *grads, vec)
 
 def own_slice(vector):
     width = vector.shape[0] // lax.axis_size("fsdp")
@@ -663,113 +1165,50 @@
     down_shift,
     cotangent,
 ):
-    dp_size, fs_size = lax.axis_size("dp"), lax.axis_size("fsdp")
-    first = first_call(dp_size, fs_size, classes, inputs, offset_table, bias_table,
+    sizes = lax.axis_size("dp"), lax.axis_size("fsdp")
+    images, _, model = inputs.shape
+
+    def by_slot(array):
+        return jnp.swapaxes(array, 0, 1).reshape(SLOT * images, model)
+
+    def by_image(array):
+        return jnp.swapaxes(array.reshape(SLOT, images, model), 0, 1)
+
+    first = first_call(
+        *sizes,
+        classes,
+        by_slot(inputs),
+        offset_table,
+        bias_table,
         (qkv_weight, out_weight, up_weight, down_weight),
-        (qkv_gain, qkv_shift, out_gain, out_shift, up_gain, up_shift, down_gain, down_shift))
-    mixed, xs, biases, weights_full, vec = first[0], first[1], first[2:5], first[5:9], first[9]
-    qkv_full, out_full, up_full, down_full = [w.reshape(-1, w.shape[2]) for w in weights_full]
-    qkv_gains, qkv_shifts = vec[0], vec[1]
-    out_gains, out_shifts = vec[2, :256], vec[3, :256]
-    up_gains, up_shifts = vec[4, :512], vec[5, :512]
-    down_gains, down_shifts = vec[6, :256], vec[7, :256]
-    total = vec[10, 0]
-    images = inputs.shape[0]
-    length = images * SLOT
-    limits = jnp.where(
-        classes == 0,
-        (GRID - 8) * (GRID - 8),
-        jnp.where(classes == 1, (GRID - 4) * (GRID - 4), SLOT),
+        (qkv_gain, qkv_shift, out_gain, out_shift, up_gain, up_shift, down_gain, down_shift),
     )
-    keep = (jnp.arange(SLOT)[None, :] < limits[:, None]).astype(jnp.float32)
-    weights = keep.reshape(-1, 1)
-    flat = inputs.reshape(length, -1)
-    z_qkv = jnp.dot(flat, qkv_full, preferred_element_type=jnp.float32)
-    hat_qkv, scale_qkv = (z_qkv - vec[9]) * vec[8], vec[8]
-    attended_low, probs, shares = attend_call(classes, mixed, biases)
-    attended = attended_low[:, :SLOT].astype(jnp.float32).reshape(length, -1)
-    activated = jax.nn.silu(attended).astype(jnp.bfloat16)
-    z_out = jnp.dot(activated, out_full, preferred_element_type=jnp.float32)
-    branch, hat_out, scale_out, unused_out = norm_forward(z_out, weights, out_gains, out_shifts)
-    middle = flat.astype(jnp.float32) + branch
-    middle_low = middle.astype(jnp.bfloat16)
-    z_up = jnp.dot(middle_low, up_full, preferred_element_type=jnp.float32)
-    up_normed, hat_up, scale_up, unused_up = norm_forward(z_up, weights, up_gains, up_shifts)
-    hidden = jax.nn.silu(up_normed).astype(jnp.bfloat16)
-    z_down = jnp.dot(hidden, down_full, preferred_element_type=jnp.float32)
-    down_normed, hat_down, scale_down, unused_down = norm_forward(
-        z_down, weights, down_gains, down_shifts
+    mixed, xs, biases, weights, vec = first[0], first[1], first[2:5], first[5:9], first[9]
+    attended, probs, shares = attend_call(classes, mixed, biases)
+    middle = middle_call(*sizes, classes, attended, xs, by_slot(cotangent), weights[1:], vec)
+    output, grad_att, grad_middle = middle[:3]
+    grad_mixed, *accs = back_call(classes, mixed, probs, shares, grad_att, attended)
+    last = last_call(
+        *sizes, classes, xs, grad_mixed, grad_middle, weights[0], offset_table, accs, middle[3:6], vec
     )
-    output = ((middle + down_normed) * weights).astype(jnp.bfloat16).reshape(inputs.shape)
-    grad_out = cotangent.astype(jnp.float32).reshape(length, -1) * weights
-    dz_down, down_gain_grad, down_shift_grad = norm_backward(
-        grad_out, hat_down, scale_down, total, down_gains, weights
-    )
-    dz_down_low = dz_down.astype(jnp.bfloat16)
-    down_grad = left_product(hidden, dz_down_low)
-    grad_up = right_product(dz_down_low, down_full) * silu_slope(up_normed)
-    dz_up, up_gain_grad, up_shift_grad = norm_backward(
-        grad_up, hat_up, scale_up, total, up_gains, weights
-    )
-    dz_up_low = dz_up.astype(jnp.bfloat16)
-    up_grad = left_product(middle_low, dz_up_low)
-    grad_middle = grad_out + right_product(dz_up_low, up_full)
-    dz_out, out_gain_grad, out_shift_grad = norm_backward(
-        grad_middle, hat_out, scale_out, total, out_gains, weights
-    )
-    dz_out_low = dz_out.astype(jnp.bfloat16)
-    out_grad = left_product(activated, dz_out_low)
-    grad_att = (right_product(dz_out_low, out_full) * silu_slope(attended)).astype(jnp.bfloat16)
-    grad_att = jnp.pad(grad_att.reshape(images, SLOT, -1), ((0, 0), (0, ROWS - SLOT), (0, 0)))
-    grad_mixed, *accs = back_call(classes, mixed, probs, shares, grad_att, attended_low)
-    local_table = table_call(offset_table, accs)[:, :NOFF]
-    grad_mixed = grad_mixed[:, :SLOT].astype(jnp.float32).reshape(length, -1)
-    dz_qkv, qkv_gain_grad, qkv_shift_grad = norm_backward(
-        grad_mixed, hat_qkv, scale_qkv, total, qkv_gains, weights
-    )
-    dz_qkv_low = dz_qkv.astype(jnp.bfloat16)
-    qkv_grad = left_product(flat, dz_qkv_low)
-    qkv_grad = restore(qkv_grad)
-    qkv_gain_grad = restore(qkv_gain_grad[None])[0]
-    qkv_shift_grad = restore(qkv_shift_grad[None])[0]
-    input_grad = (grad_middle + right_product(dz_qkv_low, qkv_full)).reshape(inputs.shape)
-    table_grad = lax.psum(local_table, ("dp", "fsdp"))
-    whole = (
-        lax.psum(qkv_grad.astype(jnp.bfloat16), "dp").astype(jnp.float32),
-        lax.psum(out_grad.astype(jnp.bfloat16), "dp").astype(jnp.float32),
-        lax.psum(up_grad.astype(jnp.bfloat16), "dp").astype(jnp.float32),
-        lax.psum(down_grad.astype(jnp.bfloat16), "dp").astype(jnp.float32),
-    )
-    summed = (
-        lax.psum_scatter(
-            whole[0].astype(jnp.bfloat16), "fsdp", scatter_dimension=0, tiled=True
-        ).astype(jnp.float32),
-        lax.psum_scatter(
-            whole[1].astype(jnp.bfloat16), "fsdp", scatter_dimension=0, tiled=True
-        ).astype(jnp.float32),
-        lax.psum_scatter(
-            whole[2].astype(jnp.bfloat16), "fsdp", scatter_dimension=0, tiled=True
-        ).astype(jnp.float32),
-        lax.psum_scatter(
-            whole[3].astype(jnp.bfloat16), "fsdp", scatter_dimension=0, tiled=True
-        ).astype(jnp.float32),
-    )
+    input_grad, table_grad, owned, vec_qkv = last[0], last[1], last[2:6], last[6]
+    lines = middle[6]
     return (
-        output,
-        input_grad,
-        table_grad,
-        summed[0],
-        own_slice(qkv_gain_grad),
-        own_slice(qkv_shift_grad),
-        summed[1],
-        own_slice(out_gain_grad),
-        own_slice(out_shift_grad),
-        summed[2],
-        own_slice(up_gain_grad),
-        own_slice(up_shift_grad),
-        summed[3],
-        own_slice(down_gain_grad),
-        own_slice(down_shift_grad),
+        by_image(output),
+        by_image(input_grad),
+        table_grad[:, :NOFF],
+        owned[0],
+        own_slice(vec_qkv[0]),
+        own_slice(vec_qkv[1]),
+        owned[1],
+        own_slice(lines[0, :model]),
+        own_slice(lines[1, :model]),
+        owned[2],
+        own_slice(lines[2]),
+        own_slice(lines[3]),
+        owned[3],
+        own_slice(lines[4, :model]),
+        own_slice(lines[5, :model]),
     )
 
 

time: 797 us -> 156 us (0.20)
  blocking collectives: 281 us -> 0 us
  waiting for transfers between devices: 251 us -> 0 us
  Pallas kernels: 66.8 us -> 135 us
  other arithmetic: 59.4 us -> 0 us
  matrix products: 48.4 us -> 0 us
  local copies, waits for them, and re-layouts: 65.4 us -> 18.6 us
  between operations: 14.4 us -> 0.75 us
    psum x7 -> x0, blocking collectives: 281 us -> none  [the longest x4 162 us: norm_backward(): lax.psum((jnp.sum(grad, axis=0), jnp.sum(grad * normed, axis=0)), ('dp',...]
    reduce_scatter x3 -> x0, waiting for transfers between devices: 189 us -> none  [the longest x1 63.6 us: shards(): lax.psum_scatter(whole[2].astype(jnp.bfloat16), 'fsdp', scatter_dimension...]
    pallas_call x1 -> x2, Pallas kernels: 5.17 us -> 75.3 us  [the longest x1 43 us: middle_call(): pl.pallas_call(functools.partial(middle_kernel, dp_size, fs_size, group),...]
    convert_element_type x13 -> x0, other arithmetic: 49.1 us -> none  [the longest x1 7.92 us: shards(): dz_qkv_low = dz_qkv.astype(jnp.bfloat16)]
    dot_general x12 -> x0, matrix products: 48.4 us -> none  [the longest x4 17.6 us: right_product(): jnp.einsum('nb,ab->na', left, right, preferred_element_type=jnp.float32)]
    psum x1 -> x0, waiting for transfers between devices: 33.3 us -> none  [shards(): lax.psum(qkv_grad.astype(jnp.bfloat16), 'dp').astype(jnp.float32)]
    unnamed x6 -> x0, waiting for transfers between devices: 29.1 us -> none
    reshape x7 -> x0, local copies, waits for them, and re-layouts: 24.3 us -> none  [the longest x1 7.3 us: shards(): grad_mixed = grad_mixed[:, :SLOT].astype(jnp.float32).reshape(length, -1)]
  transfers between devices with their start and end apart: 5 -> 0, of which waited for: 5 -> 0; matrix products, arithmetic and copies ran while one was open for 4% -> 0% of each run, Pallas kernels for 0% -> 0%
where the time goes in v3:
time: 156 us; the launch traced here: 154 us
  Pallas kernels  135 us (87%)
  local copies, waits for them, and re-layouts  18.6 us (12%)
    pallas_call x1, Pallas kernels, middle_call(): pl.pallas_call(functools.partial(middle_kernel, dp_size, fs_size, group),...  43 us
    pallas_call x1, Pallas kernels, first_call(): pl.pallas_call(functools.partial(first_kernel, dp_size, fs_size), out_sha...  32.6 us
    pallas_call x1, Pallas kernels, last_call(): pl.pallas_call(functools.partial(last_kernel, dp_size, fs_size, group), o...  32.3 us
    pallas_call x1, Pallas kernels, back_call(): pl.pallas_call(back_kernel, grid_spec=pltpu.PrefetchScalarGridSpec(num_sc...  15.6 us
    unnamed x35, local copies, waits for them, and re-layouts  13.7 us
    pallas_call x1, Pallas kernels, attend_call(): pl.pallas_call(attend_kernel, grid_spec=pltpu.PrefetchScalarGridSpec(num_...  11.2 us

profile of v3, /device:TPU:0, one launch (start us, length us, event | category | flops | bytes accessed | tf_op | source)
XLA Modules:
  0.0 154.1 jit_solution(17453197116240971572)
XLA Ops:
  0.7 0.0 copy-start.6
  0.7 32.6 %shard_map.280 = (bf16[8,336,768]{2,1,0:T(8,128)(2,1)}, bf16[8,336,256]{2,1,0:T(8,128)(2,1)}, f32[2,112,256]{2,1,0:T(8,128)}, f32[2,208,512]{2,1,0:T(8,128)}, f3...) custom-call(s32[8]{0:T(128)} %refs_0_.5, ...), custom_call_target="tpu_custom_call" | custom-call | tf_op jit(solution)/shard_map/pallas_call | solution.py:564
  33.2 0.0 copy-done.6
  33.2 0.0 copy-start
  33.2 1.6 %copy-done = f32[2,336,768]{2,1,0:T(8,128)S(1)} copy-done((f32[2,336,768]{2,1,0:T(8,128)S(1)}, f32[2,336,768]{2,1,0:T(8,128)}, u32[]{:S(2)}) %copy-start) | copy-done | bytes 2064408
  34.8 1.2 copy-done.2
  36.0 0.9 copy-done.4
  36.9 11.2 %shard_map.281 = (bf16[8,336,512]{2,1,0:T(8,128)(2,1)}, bf16[8,336,1536]{2,1,0:T(8,128)(2,1)}, f32[8,336,128]{2,1,0:T(8,128)S(1)}) custom-call(s32[8]{0:T(128)S(1)} %copy-done.6, bf16[8,336,768]{2,1,0:T(8,128)(2,1)} %get-tuple-element.46.mixed_ref, f32[2,112,256]{2,1,0:T(8,128)S(1)} %copy-done.4, f32[2,208,512]{2,1,0:T(8,128)S(1)} %copy-done.2, ...), custom_call_target="tpu_custom_call" | custom-call | tf_op jit(solution)/shard_map/pallas_call | solution.py:241
  48.2 43.0 %shard_map.282 = (bf16[2592,256]{1,0:T(8,128)(2,1)}, bf16[8,336,512]{2,1,0:T(8,128)(2,1)}, f32[8,336,256]{2,1,0:T(8,128)}, bf16[8,64,256]{2,1,0:T(8,128)(2,1)}, ...) custom-call(s32[8]{0:T(128)} %refs_0_.5, ...), custom_call_target="tpu_custom_call" | custom-call | tf_op jit(solution)/shard_map/pallas_call | solution.py:872
  91.1 0.9 fusion.9
  92.0 0.6 fusion.6
  92.6 0.8 fusion.10
  93.4 0.6 fusion.4
  94.0 0.6 fusion.2
  94.6 0.0 copy-done.7
  94.6 15.6 %shard_map.283 = (bf16[8,336,768]{2,1,0:T(8,128)(2,1)}, f32[2,112,256]{2,1,0:T(8,128)S(1)}, f32[2,208,512]{2,1,0:T(8,128)S(1)}, f32[2,336,768]{2,1,0:T(8,128)S(1)}) custom-call(s32[8]{0:T(128)S(1)} %copy-done.7, bf16[8,336,768]{2,1,0:T(8,128)(2,1)} %get-tuple-element.46.mixed_ref, bf16[8,336,1536]{2,1,0:T(8,128)(2,1)} %get-tuple-element.57.p_ref, ...), custom_call_target="tpu_custom_call" | custom-call | tf_op jit(solution)/shard_map/pallas_call | solution.py:261
  110.2 1.3 copy-done.1
  111.5 0.9 copy-done.3
  112.4 0.7 copy-done.5
  113.1 32.3 %shard_map.284 = (f32[2592,256]{1,0:T(8,128)}, f32[4,384]{1,0:T(4,128)}, f32[32,768]{1,0:T(8,128)}, f32[64,256]{1,0:T(8,128)}, f32[32,512]{1,0:T(8,128)}, /*index=5*/f32[64,256]{1,0:T(8,128)}, f32[8,768]{1,0:T(8,128)}) custom-call(s32[8]{0:T(128)} %refs_0_.5, bf16[8,336,256]{2,1,0:T(8,128)(2,1)} %get-tuple-element.51.refs_2_.refs_1_, ...), custom_call_target="tpu_custom_call" | custom-call | tf_op jit(solution)/shard_map/pallas_call | solution.py:1111
  145.4 0.0 copy-start.8
  145.5 0.9 fusion.8
  146.4 0.6 fusion
  147.0 2.5 %copy.39 = bf16[8,324,256]{2,0,1:T(8,128)(2,1)} copy(bf16[8,324,256]{2,0,1:T(8,128)(2,1)} %bitcast.38) | data formatting | bytes 2654208
  149.4 0.0 copy-done.8
  149.4 0.0 copy-start.11
  149.5 1.5 copy.40
  151.0 0.6 copy.41
  151.6 0.6 copy.42
  152.2 0.6 copy.43
  152.8 0.6 copy.44
  153.5 0.6 copy.45
  (15 shorter events, 0.0 us)
Async XLA Ops:
  0.7 32.6 %copy-start.6 = (s32[8]{0:T(128)S(1)}, s32[8]{0:T(128)}, u32[]{:S(2)}) copy-start(s32[8]{0:T(128)} %refs_0_.5) | copy-start | bytes 100
  33.2 1.6 %copy-start = (f32[2,336,768]{2,1,0:T(8,128)S(1)}, f32[2,336,768]{2,1,0:T(8,128)}, u32[]{:S(2)}) copy-start(f32[2,336,768]{2,1,0:T(8,128)} %get-tuple-element.49.bias2) | copy-start | bytes 6193156
  34.8 1.2 copy-start.2
  36.0 0.9 copy-start.4
  48.2 46.4 %copy-start.7 = (s32[8]{0:T(128)S(1)}, s32[8]{0:T(128)}, u32[]{:S(2)}) copy-start(s32[8]{0:T(128)} %refs_0_.5) | copy-start | bytes 100
  110.2 1.3 copy-start.1
  111.5 0.9 copy-start.3
  112.4 0.7 copy-start.5
  145.4 4.0 %copy-start.8 = (f32[2592,256]{1,0:T(8,128)S(1)}, f32[2592,256]{1,0:T(8,128)}, u32[]{:S(2)}) copy-start(f32[2592,256]{1,0:T(8,128)} %get-tuple-element.69) | copy-start | bytes 7962628
  149.4 1.5 copy-start.13
  149.4 2.1 %copy-start.9 = (f32[32,768]{1,0:T(8,128)S(1)}, f32[32,768]{1,0:T(8,128)}, u32[]{:S(2)}) copy-start(f32[32,768]{1,0:T(8,128)} %get-tuple-element.111) | copy-start | bytes 294916
  149.4 2.8 %copy-start.12 = (f32[64,256]{1,0:T(8,128)S(1)}, f32[64,256]{1,0:T(8,128)}, u32[]{:S(2)}) copy-start(f32[64,256]{1,0:T(8,128)} %get-tuple-element.114) | copy-start | bytes 196612
  149.4 3.4 %copy-start.11 = (f32[32,512]{1,0:T(8,128)S(1)}, f32[32,512]{1,0:T(8,128)}, u32[]{:S(2)}) copy-start(f32[32,512]{1,0:T(8,128)} %get-tuple-element.117) | copy-start | bytes 196612
  149.4 4.0 %copy-start.10 = (f32[64,256]{1,0:T(8,128)S(1)}, f32[64,256]{1,0:T(8,128)}, u32[]{:S(2)}) copy-start(f32[64,256]{1,0:T(8,128)} %get-tuple-element.120) | copy-start | bytes 196612
